TPU v7x, 32 devices: a whole 2x2x4 slice. The times are simulated.
32 devices in a mesh: clip: 8 (over y, x, core), frame: 4 (over z).
Axes of the slice: x: 2, y: 2, z: 4, core: 2. Of those that a mesh axis runs over, the one named last changes fastest.
Arguments:
- layer_input: bfloat16 [4096, 768], P(('clip', 'frame')), may hold values from -6 to 6
- first_gain: bfloat16 [768], P(('clip', 'frame')), may hold values from 0.5 to 1.5
- first_bias: bfloat16 [768], P(('clip', 'frame')), may hold values from -3 to 3
- query_weight: bfloat16 [768, 768], P(('clip', 'frame')), may hold values from -0.21875 to 0.21875
- query_bias: bfloat16 [768], P(('clip', 'frame')), may hold values from -3 to 3
- key_weight: bfloat16 [768, 768], P(('clip', 'frame')), may hold values from -0.21875 to 0.21875
- value_weight: bfloat16 [768, 768], P(('clip', 'frame')), may hold values from -0.21875 to 0.21875
- value_bias: bfloat16 [768], P(('clip', 'frame')), may hold values from -3 to 3
- output_weight: bfloat16 [768, 768], P(('clip', 'frame')), may hold values from -1.75 to 1.75
- output_bias: bfloat16 [768], P(('clip', 'frame')), may hold values from -3 to 3
- second_gain: bfloat16 [768], P(('clip', 'frame')), may hold values from 0.5 to 1.5
- second_bias: bfloat16 [768], P(('clip', 'frame')), may hold values from -3 to 3
- inner_weight: bfloat16 [768, 3072], P(('clip', 'frame')), may hold values from -0.21875 to 0.21875
- inner_bias: bfloat16 [3072], P(('clip', 'frame')), may hold values from -3 to 3
- outer_weight: bfloat16 [3072, 768], P(('clip', 'frame')), may hold values from -0.15625 to 0.15625
- outer_bias: bfloat16 [768], P(('clip', 'frame')), may hold values from -3 to 3
- upstream: bfloat16 [4096, 768], P(('clip', 'frame')), may hold values from -6 to 6
Outputs:
- layer_output: bfloat16 [4096, 768], P(('clip', 'frame'))
- input_grad: bfloat16 [4096, 768], P(('clip', 'frame'))
- grad_first_gain: float32 [768], P(('clip', 'frame'))
- grad_first_bias: float32 [768], P(('clip', 'frame'))
- grad_query_weight: float32 [768, 768], P(('clip', 'frame'))
- grad_query_bias: float32 [768], P(('clip', 'frame'))
- grad_key_weight: float32 [768, 768], P(('clip', 'frame'))
- grad_value_weight: float32 [768, 768], P(('clip', 'frame'))
- grad_value_bias: float32 [768], P(('clip', 'frame'))
- grad_output_weight: float32 [768, 768], P(('clip', 'frame'))
- grad_output_bias: float32 [768], P(('clip', 'frame'))
- grad_second_gain: float32 [768], P(('clip', 'frame'))
- grad_second_bias: float32 [768], P(('clip', 'frame'))
- grad_inner_weight: float32 [768, 3072], P(('clip', 'frame'))
- grad_inner_bias: float32 [3072], P(('clip', 'frame'))
- grad_outer_weight: float32 [3072, 768], P(('clip', 'frame'))
- grad_outer_bias: float32 [768], P(('clip', 'frame'))
All inputs are finite; a program needn't handle non-finite values.
Results may differ from a plain program's by a relative error of at most 0.012.
The roundings to bfloat16 on the way count: a program that leaves them out, or rounds other values in their place, can miss the bound.
Values may be sent and summed in bfloat16 or wider, within the bound.
A program may use at most 192 MiB of HBM per device.

v0:
```python
import jax
import jax.numpy as jnp
from jax import lax
from jax.sharding import PartitionSpec as P

HEADS = 12
HEAD_DIM = 64


EPS = 1e-05
SQRT_HALF = 0.7071067811865476
INV_ROOT = 0.3989422804014327


def for_sending(array):

    def short(part):
        return part.astype(jnp.bfloat16) if part.dtype == jnp.float32 else part

    return jax.tree.map(short, array)


def normalize(rows):
    mean = jnp.mean(rows, axis=-1, keepdims=True)
    centered = rows - mean
    rstd = lax.rsqrt(jnp.mean(centered * centered, axis=-1, keepdims=True) + EPS)
    return (centered * rstd, rstd)


def norm_back(grad_norm, normed, rstd):
    first = jnp.mean(grad_norm, axis=-1, keepdims=True)
    second = jnp.mean(grad_norm * normed, axis=-1, keepdims=True)
    return rstd * (grad_norm - first - normed * second)


def gelu_slope(inner):
    return (
        0.5 * (1.0 + lax.erf(inner * SQRT_HALF)) + inner * jnp.exp(-0.5 * inner * inner) * INV_ROOT
    )


def matmul(left, right):
    return jnp.dot(left, right, preferred_element_type=jnp.float32)


def left_product(left, right):
    return jnp.einsum("ti,to->io", left, right, preferred_element_type=jnp.float32)


def right_product(left, right):
    return jnp.einsum("to,io->ti", left, right, preferred_element_type=jnp.float32)


def flatten(items):
    return tuple((item.reshape(-1) for item in items))


def unflatten(flats, shapes):
    return tuple((flat.reshape((-1,) + shape[1:]) for flat, shape in zip(flats, shapes)))


def collect(params):
    shapes = [item.shape for item in params]
    flats = flatten(params)
    whole = jax.tree.map(
        lambda part, own: part.astype(own.dtype),
        lax.all_gather(for_sending(flats), ("clip", "frame"), axis=0, tiled=True),
        flats,
    )
    return unflatten(whole, shapes)


def spread(grads):
    shapes = [item.shape for item in grads]
    flats = flatten(grads)
    owned = lax.psum_scatter(flats, ("clip", "frame"), scatter_dimension=0, tiled=True)
    return unflatten(owned, shapes)


def body(
    layer_input,
    first_gain,
    first_bias,
    query_weight,
    query_bias,
    key_weight,
    value_weight,
    value_bias,
    output_weight,
    output_bias,
    second_gain,
    second_bias,
    inner_weight,
    inner_bias,
    outer_weight,
    outer_bias,
    upstream,
):
    f32 = jnp.float32
    bf16 = jnp.bfloat16
    scale = HEAD_DIM ** (-0.5)
    params = (
        first_gain,
        first_bias,
        query_weight,
        query_bias,
        key_weight,
        value_weight,
        value_bias,
        output_weight,
        output_bias,
        second_gain,
        second_bias,
        inner_weight,
        inner_bias,
        outer_weight,
        outer_bias,
    )
    (
        pre_gain,
        pre_shift,
        query_mat,
        query_add,
        key_mat,
        value_mat,
        value_add,
        proj_mat,
        proj_add,
        post_gain,
        post_shift,
        inner_mat,
        inner_add,
        outer_mat,
        outer_add,
    ) = collect(params)
    local = layer_input.shape[0]
    width = layer_input.shape[1]
    rows = layer_input.astype(f32)
    first_norm, first_rstd = normalize(rows)
    first_hidden = (first_norm * pre_gain.astype(f32) + pre_shift.astype(f32)).astype(bf16)
    queries = ((matmul(first_hidden, query_mat) + query_add.astype(f32)) * scale).astype(bf16)
    keys = matmul(first_hidden, key_mat).astype(bf16)
    values = (matmul(first_hidden, value_mat) + value_add.astype(f32)).astype(bf16)
    all_keys, all_values = (
        lax.all_gather(keys, "frame", axis=0, tiled=True),
        lax.all_gather(values, "frame", axis=0, tiled=True),
    )
    q_heads = queries.reshape(local, HEADS, HEAD_DIM)
    k_heads = all_keys.reshape(-1, HEADS, HEAD_DIM)
    v_heads = all_values.reshape(-1, HEADS, HEAD_DIM)
    scores = jnp.einsum("qhd,khd->hqk", q_heads, k_heads, preferred_element_type=f32)
    log_total = jax.nn.logsumexp(scores, axis=-1, keepdims=True)
    probs = jnp.exp(scores - log_total).astype(bf16)
    attended = (
        jnp.einsum("hqk,khd->qhd", probs, v_heads, preferred_element_type=f32)
        .reshape(local, width)
        .astype(bf16)
    )
    middle = rows + matmul(attended, proj_mat) + proj_add.astype(f32)
    second_norm, second_rstd = normalize(middle)
    second_hidden = (second_norm * post_gain.astype(f32) + post_shift.astype(f32)).astype(bf16)
    inner = matmul(second_hidden, inner_mat) + inner_add.astype(f32)
    activated = jax.nn.gelu(inner, approximate=False).astype(bf16)
    layer_output = (middle + matmul(activated, outer_mat) + outer_add.astype(f32)).astype(bf16)
    (
        pre_gain,
        pre_shift,
        query_mat,
        query_add,
        key_mat,
        value_mat,
        value_add,
        proj_mat,
        proj_add,
        post_gain,
        post_shift,
        inner_mat,
        inner_add,
        outer_mat,
        outer_add,
    ) = collect(params)
    grad_out = upstream.astype(f32)
    g_outer_w = left_product(activated, upstream)
    g_outer_b = jnp.sum(grad_out, axis=0)
    grad_inner = right_product(upstream, outer_mat) * gelu_slope(inner)
    inner_round = grad_inner.astype(bf16)
    g_inner_w = left_product(second_hidden, inner_round)
    g_inner_b = jnp.sum(grad_inner, axis=0)
    grad_second = right_product(inner_round, inner_mat)
    g_second_g = jnp.sum(grad_second * second_norm, axis=0)
    g_second_b = jnp.sum(grad_second, axis=0)
    grad_middle = grad_out + norm_back(
        grad_second * post_gain.astype(f32), second_norm, second_rstd
    )
    middle_round = grad_middle.astype(bf16)
    g_proj_w = left_product(attended, middle_round)
    g_proj_b = jnp.sum(grad_middle, axis=0)
    grad_attended = right_product(middle_round, proj_mat).astype(bf16)
    scores = jnp.einsum("qhd,khd->hqk", q_heads, k_heads, preferred_element_type=f32)
    chance = jnp.exp(scores - log_total)
    again_probs = chance.astype(bf16)
    g_heads = grad_attended.reshape(local, HEADS, HEAD_DIM)
    a_heads = attended.reshape(local, HEADS, HEAD_DIM)
    grad_probs = jnp.einsum("qhd,khd->hqk", g_heads, v_heads, preferred_element_type=f32)
    offsets = jnp.einsum("qhd,qhd->hq", g_heads, a_heads, preferred_element_type=f32)[:, :, None]
    grad_scores = (chance * (grad_probs - offsets)).astype(bf16)
    grad_queries = (
        jnp.einsum("hqk,khd->qhd", grad_scores, k_heads, preferred_element_type=f32) * scale
    ).reshape(local, width)
    key_terms = jnp.einsum(
        "hqk,qhd->khd", grad_scores, q_heads, preferred_element_type=f32
    ).reshape(-1, width)
    value_terms = jnp.einsum(
        "hqk,qhd->khd", again_probs, g_heads, preferred_element_type=f32
    ).reshape(-1, width)
    grad_keys, grad_values = (
        lax.psum_scatter(key_terms, "frame", scatter_dimension=0, tiled=True),
        lax.psum_scatter(value_terms, "frame", scatter_dimension=0, tiled=True),
    )
    query_round = grad_queries.astype(bf16)
    key_round = grad_keys.astype(bf16)
    value_round = grad_values.astype(bf16)
    g_query_w = left_product(first_hidden, query_round)
    g_key_w = left_product(first_hidden, key_round)
    g_value_w = left_product(first_hidden, value_round)
    g_query_b = jnp.sum(grad_queries, axis=0)
    g_value_b = jnp.sum(grad_values, axis=0)
    grad_first = (
        right_product(query_round, query_mat)
        + right_product(key_round, key_mat)
        + right_product(value_round, value_mat)
    )
    g_first_g = jnp.sum(grad_first * first_norm, axis=0)
    g_first_b = jnp.sum(grad_first, axis=0)
    input_grad = (
        grad_middle + norm_back(grad_first * pre_gain.astype(f32), first_norm, first_rstd)
    ).astype(bf16)
    owned = spread(
        (
            g_first_g,
            g_first_b,
            g_query_w,
            g_query_b,
            g_key_w,
            g_value_w,
            g_value_b,
            g_proj_w,
            g_proj_b,
            g_second_g,
            g_second_b,
            g_inner_w,
            g_inner_b,
            g_outer_w,
            g_outer_b,
        )
    )
    return (
        layer_output,
        input_grad,
        owned[0],
        owned[1],
        owned[2],
        owned[3],
        owned[4],
        owned[5],
        owned[6],
        owned[7],
        owned[8],
        owned[9],
        owned[10],
        owned[11],
        owned[12],
        owned[13],
        owned[14],
    )


def solution(mesh):
    placed = (
        P(("clip", "frame"), None),
        P(("clip", "frame")),
        P(("clip", "frame")),
        P(("clip", "frame"), None),
        P(("clip", "frame")),
        P(("clip", "frame"), None),
        P(("clip", "frame"), None),
        P(("clip", "frame")),
        P(("clip", "frame"), None),
        P(("clip", "frame")),
        P(("clip", "frame")),
        P(("clip", "frame")),
        P(("clip", "frame"), None),
        P(("clip", "frame")),
        P(("clip", "frame"), None),
        P(("clip", "frame")),
        P(("clip", "frame"), None),
    )
    return jax.shard_map(
        body,
        mesh=mesh,
        in_specs=placed,
        out_specs=(
            P(("clip", "frame"), None),
            P(("clip", "frame"), None),
            P(("clip", "frame")),
            P(("clip", "frame")),
            P(("clip", "frame"), None),
            P(("clip", "frame")),
            P(("clip", "frame"), None),
            P(("clip", "frame"), None),
            P(("clip", "frame")),
            P(("clip", "frame"), None),
            P(("clip", "frame")),
            P(("clip", "frame")),
            P(("clip", "frame")),
            P(("clip", "frame"), None),
            P(("clip", "frame")),
            P(("clip", "frame"), None),
            P(("clip", "frame")),
        ),
        check_vma=False,
    )
```

profile of v0, /device:TPU:0, one launch (start us, length us, event | category | flops | bytes accessed | tf_op | source)
XLA Modules:
  0.0 922.7 jit_solution(1836691230997473496)
XLA Ops:
  7.2 1.5 reshape.213
  8.8 1.4 reshape.216
  10.3 1.4 reshape.210
  11.8 1.4 reshape.219
  13.3 1.6 copy.59
  15.0 1.7 reshape.223
  16.8 0.8 dynamic-update-slice.5
  21.0 0.8 dynamic-update-slice.1
  21.8 0.8 dynamic-update-slice.2
  23.5 0.8 dynamic-update-slice.7
  24.4 42.7 %all-reduce.26 = (bf16[768]{0:T(1024)(128)(2,1)S(1)}, bf16[768]{0:T(1024)(128)(2,1)S(1)}, bf16[768]{0:T(1024)(128)(2,1)S(1)}, bf16[768]{0:T(1024)(128)(2,1)S(1)}...) all-reduce(bf16[768]{0:T(1024)(128)(2,1)S(1)} %dynamic-update-slice, ...), channel_id=1, replica_groups=mesh['clip'=8,'frame'=4] {'clip','frame'}, use_global_device_ids=true, to_apply=%add.2 | all-reduce | flops 9216 | bytes 36864
  69.2 2.6 reshape.214
  73.1 51.7 %all-gather.11.cloned.1.call-done = bf16[589824]{0:T(1024)(128)(2,1)} async-done(((bf16[18432]{0:T(1024)(128)(2,1)}), bf16[589824]{0:T(1024)(128)(2,1)}) %all-gather.11.cloned.1.call-update) | async-done | bytes 1179664 | tf_op jit(solution)/shard_map/all_gather | solution.py:67
  124.8 2.6 reshape.217
  127.8 18.8 %all_gather.67 = bf16[512,768]{1,0:T(8,128)(2,1)S(1)} all-gather(bf16[128,768]{1,0:T(8,128)(2,1)S(1)} %convolution_convert_fusion.2), channel_id=1, replica_groups=mesh['clip'=8,'frame'=4] {'frame'}, dimensions={0}, use_global_device_ids=true | all-gather | bytes 983040 | tf_op jit(solution)/shard_map/all_gather | solution.py:145
  146.6 1.2 copy.48
  147.8 33.8 %all-gather.7.cloned.1.call-done = bf16[589824]{0:T(1024)(128)(2,1)} async-done(((bf16[18432]{0:T(1024)(128)(2,1)}), bf16[589824]{0:T(1024)(128)(2,1)}) %all-gather.7.cloned.1.call-update) | async-done | bytes 1179664 | tf_op jit(solution)/shard_map/all_gather | solution.py:67
  181.6 2.6 reshape.211
  184.6 19.1 %all_gather.63 = bf16[512,768]{1,0:T(8,128)(2,1)S(1)} all-gather(bf16[128,768]{1,0:T(8,128)(2,1)S(1)} %fusion.21), channel_id=1, replica_groups=mesh['clip'=8,'frame'=4] {'frame'}, dimensions={0}, use_global_device_ids=true | all-gather | bytes 983040 | tf_op jit(solution)/shard_map/all_gather | solution.py:146
  203.7 1.2 copy.46
  204.9 33.4 %all-gather.13.cloned.1.call-done = bf16[589824]{0:T(1024)(128)(2,1)} async-done(((bf16[18432]{0:T(1024)(128)(2,1)}), bf16[589824]{0:T(1024)(128)(2,1)}) %all-gather.13.cloned.1.call-update) | async-done | bytes 1179664 | tf_op jit(solution)/shard_map/all_gather | solution.py:67
  238.3 3.3 reshape.220
  241.7 1.8 fusion.62
  243.5 0.8 exponential_reduce_fusion
  247.7 56.3 %all-gather.15.cloned.1.call-done = bf16[2359296]{0:T(1024)(128)(2,1)} async-done(((bf16[73728]{0:T(1024)(128)(2,1)}), bf16[2359296]{0:T(1024)(128)(2,1)}) %all-gather.15.cloned.1.call-update) | async-done | bytes 4718608 | tf_op jit(solution)/shard_map/all_gather | solution.py:67
  304.1 8.2 reshape.222
  312.3 7.9 fusion.3
  320.2 49.5 %all-gather.17.cloned.1.call-done = bf16[2359296]{0:T(1024)(128)(2,1)} async-done(((bf16[73728]{0:T(1024)(128)(2,1)}), bf16[2359296]{0:T(1024)(128)(2,1)}) %all-gather.17.cloned.1.call-update) | async-done | bytes 4718608 | tf_op jit(solution)/shard_map/all_gather | solution.py:67
  369.7 9.2 %reshape.224 = bf16[3072,768]{1,0:T(8,128)(2,1)} reshape(bf16[2359296]{0:T(1024)(128)(2,1)} %all-gather.17.cloned.1.call-done) | data formatting | bytes 9437184 | tf_op jit(solution)/shard_map/reshape | solution.py:59
  378.9 5.4 fusion.64
  384.3 2.3 multiply_reduce_fusion
  388.3 1.2 convolution_convert_fusion
  389.5 1.7 copy.49
  391.2 2.9 fusion.28
  394.2 1.1 fusion.40
  395.3 2.2 multiply_convert_fusion
  397.5 1.7 fusion.66
  399.3 0.9 copy-done.11
  400.2 1.9 fusion.50
  402.1 3.4 reshape.234
  405.6 1.3 fusion.61
  407.5 1.6 reshape.228
  409.1 2.7 convolution_bitcast_fusion
  411.8 5.9 copy.60
  417.7 5.1 fusion.67
  422.8 10.8 %reshape.238 = f32[2359296]{0:T(1024)} reshape(f32[3072,768]{1,0:T(8,128)} %fusion.67) | data formatting | bytes 18874368 | tf_op jit(solution)/shard_map/reshape | solution.py:55
  433.6 1.6 fusion.44
  435.2 1.5 reshape.232
  436.7 28.3 %reduce-scatter.3.cloned.1.call-done = f32[128,768]{0,1:T(8,128)} async-done(((f32[512,768]{0,1:T(8,128)}), f32[128,768]{0,1:T(8,128)}) %reduce-scatter.3.cloned.1.call-update) | async-done | bytes 393232 | tf_op jit(solution)/shard_map/reduce_scatter | solution.py:217
  465.0 1.6 fusion.47
  466.6 1.6 reshape.230
  469.5 1.3 fusion.65
  470.8 3.9 fusion.19
  474.7 1.3 reduce_sum.177
  476.0 1.9 convolution_add_fusion.2
  478.7 41.7 %all-reduce.24 = (f32[768]{0:T(1024)S(1)}, f32[768]{0:T(1024)S(1)}, f32[768]{0:T(1024)S(1)}, f32[768]{0:T(1024)S(1)}, f32[768]{0:T(1024)S(1)}, /*index=5*/f32[76...) all-reduce(f32[768]{0:T(1024)S(1)} %get-tuple-element.19, ...), channel_id=4, replica_groups=mesh['clip'=8,'frame'=4] {'clip','frame'}, use_global_device_ids=true, to_apply=%region_13.0.clone | all-reduce | flops 9216 | bytes 73728
  525.7 0.9 fusion.37
  526.5 380.0 %all-reduce.29.cloned.1.call-done = (f32[589824]{0:T(1024)}, f32[589824]{0:T(1024)}, f32[589824]{0:T(1024)}, f32[589824]{0:T(1024)}, f32[2359296]{0:T(1024)}, /*index=5*/f32[2359296]{0:T(1024)}) async-done(((f32[589824]{0:T(1024)}, f32[589824]{0:T(1024)}, f32[589824]{0:T(1024)}, f32[589824]{0:T(1024)}, f32[2359296]{0:T(1024)}, /*index=5*/f32[2359296]{0:T(1024)}), (f32[589824]{0:T(1024)}, f32[589824]{0:T(1024)}, ...) | async-done | bytes 28311568
  906.6 0.9 dynamic-slice.2
  908.1 0.9 dynamic-slice.4
  909.6 0.9 dynamic-slice.5
  910.5 0.9 dynamic-slice.7
  912.7 1.0 dynamic-slice.11
  913.7 1.0 dynamic-slice.13
  (177 shorter events, 25.9 us)
Async XLA Ops:
  7.2 61.7 %copy-start.3 = (bf16[128,768]{1,0:T(8,128)(2,1)S(1)}, bf16[128,768]{1,0:T(8,128)(2,1)}, u32[]{:S(2)}) copy-start(bf16[128,768]{1,0:T(8,128)(2,1)} %param.17) | copy-start | bytes 589828
  7.2 62.0 %all-gather.9.cloned.1.call-start = ((), (), s32[]{:S(2)}) async-start(), calls=%async_computation.3 | async-start | bytes 1216512 | tf_op jit(solution)/shard_map/all_gather | solution.py:67
  8.7 116.0 %all-gather.11.cloned.1.call-start = ((), (), s32[]{:S(2)}) async-start(), calls=%async_computation.4 | async-start | bytes 1216512 | tf_op jit(solution)/shard_map/all_gather | solution.py:67
  10.3 171.4 %all-gather.7.cloned.1.call-start = ((), (), s32[]{:S(2)}) async-start(), calls=%async_computation.2 | async-start | bytes 1216512 | tf_op jit(solution)/shard_map/all_gather | solution.py:67
  11.8 226.6 %all-gather.13.cloned.1.call-start = ((), (), s32[]{:S(2)}) async-start(), calls=%async_computation.5 | async-start | bytes 1216512 | tf_op jit(solution)/shard_map/all_gather | solution.py:67
  13.3 290.8 %all-gather.15.cloned.1.call-start = ((), (), s32[]{:S(2)}) async-start(), calls=%async_computation.6 | async-start | bytes 4866048 | tf_op jit(solution)/shard_map/all_gather | solution.py:67
  14.9 354.8 %all-gather.17.cloned.1.call-start = ((), (), s32[]{:S(2)}) async-start(), calls=%async_computation.7 | async-start | bytes 4866048 | tf_op jit(solution)/shard_map/all_gather | solution.py:67
  16.7 416.9 %reduce-scatter.5.cloned.1.call-start = ((), (), s32[]{:S(2)}) async-start(), calls=%async_computation.9 | async-start | bytes 1966080 | tf_op jit(solution)/shard_map/reduce_scatter | solution.py:218
  67.1 117.2 %copy-start.29 = (f32[768]{0:T(1024)}, f32[768]{0:T(1024)S(1)}, u32[]{:S(2)}) copy-start(f32[768]{0:T(1024)S(1)} %convert_element_type.102) | copy-start | bytes 9220
  69.0 115.2 %copy-start.32 = (f32[128]{0:T(128)}, f32[128]{0:T(128)S(1)}, u32[]{:S(2)}) copy-start(f32[128]{0:T(128)S(1)} %broadcast_multiply_fusion.5) | copy-start | bytes 1540
  69.2 115.0 %copy-start.42 = (f32[128]{0:T(128)}, f32[128]{0:T(128)S(1)}, u32[]{:S(2)}) copy-start(f32[128]{0:T(128)S(1)} %add_rsqrt_fusion.1) | copy-start | bytes 1540
  71.8 55.5 %copy-start.12 = (bf16[768,768]{1,0:T(8,128)(2,1)}, bf16[768,768]{1,0:T(8,128)(2,1)S(1)}, u32[]{:S(2)}) copy-start(bf16[768,768]{1,0:T(8,128)(2,1)S(1)} %reshape.214) | copy-start | bytes 3538948
  127.4 20.4 %copy-start.14 = (bf16[768,768]{1,0:T(8,128)(2,1)}, bf16[768,768]{1,0:T(8,128)(2,1)S(1)}, u32[]{:S(2)}) copy-start(bf16[768,768]{1,0:T(8,128)(2,1)S(1)} %reshape.217) | copy-start | bytes 3538948
  184.2 20.6 %copy-start.16 = (bf16[768,768]{1,0:T(8,128)(2,1)}, bf16[768,768]{1,0:T(8,128)(2,1)S(1)}, u32[]{:S(2)}) copy-start(bf16[768,768]{1,0:T(8,128)(2,1)S(1)} %reshape.211) | copy-start | bytes 3538948
  204.9 36.8 %copy-start.24 = (bf16[128,768]{0,1:T(8,128)(2,1)S(1)}, bf16[128,768]{0,1:T(8,128)(2,1)}, u32[]{:S(2)}) copy-start(bf16[128,768]{0,1:T(8,128)(2,1)} %copy.47) | copy-start | bytes 589828
  243.5 1.1 copy-start.9
  244.6 0.9 copy-start.4
  244.7 1.4 copy-start.6
  244.7 1.4 copy-start.35
  245.4 1.0 copy-start.21
  246.5 0.5 copy-start.40
  378.9 5.4 copy-start
  378.9 5.4 copy-start.41
  378.9 5.4 copy-start.47
  384.3 2.4 copy-start.23
  384.3 2.3 copy-start.26
  386.7 1.6 copy-start.7
  387.5 0.8 copy-start.10
  394.2 70.9 %reduce-scatter.3.cloned.1.call-start = ((), (), s32[]{:S(2)}) async-start(), calls=%async_computation.8 | async-start | bytes 1966080 | tf_op jit(solution)/shard_map/reduce_scatter | solution.py:217
  395.3 2.2 copy-start.25
  397.5 1.7 copy-start.1
  399.2 1.0 copy-start.11
  399.2 1.1 copy-start.22
  399.2 507.3 %all-reduce.29.cloned.1.call-start = ((), (), s32[]{:S(2)}) async-start(), calls=%async_computation.10 | async-start | bytes 56623104
  402.1 3.4 copy-start.2
  402.1 3.4 copy-start.8
  405.5 1.4 copy-start.5
  405.5 1.4 copy-start.30
  405.5 1.4 copy-start.33
  405.5 1.3 copy-start.43
  407.5 1.6 copy-start.28
  411.8 5.9 copy-start.18
  411.8 5.9 copy-start.27
  422.8 10.8 %copy-start.34 = (f32[128]{0:T(128)S(1)}, f32[128]{0:T(128)}, u32[]{:S(2)}) copy-start(f32[128]{0:T(128)} %copy-done.32) | copy-start | bytes 1540
  422.8 10.8 %copy-start.44 = (f32[128]{0:T(128)S(1)}, f32[128]{0:T(128)}, u32[]{:S(2)}) copy-start(f32[128]{0:T(128)} %copy-done.42) | copy-start | bytes 1540
  468.2 0.7 copy-start.48
  468.2 0.7 copy-start.31
  468.2 1.3 copy-start.13
  468.2 2.5 copy-start.19
  470.8 5.2 copy-start.15
  474.7 3.2 copy-start.17
  474.7 3.2 copy-start.20
  474.7 3.2 copy-start.45
  477.9 0.7 copy-start.36
  477.9 0.7 copy-start.37
  477.9 0.7 copy-start.38
  478.0 0.7 copy-start.39
  478.0 0.7 copy-start.46
Sparse Core Ops, SparseCore 0:
  11.4 56.8 all-gather.8
  71.7 53.0 all-gather.10
  128.2 53.4 all-gather.6
  184.9 53.4 all-gather.12
  241.5 62.4 all-gather.14
  307.3 62.3 all-gather.16
  394.3 34.0 reduce-scatter.4
  430.7 34.2 reduce-scatter.2
  471.5 435.0 all-reduce.28
where the time goes:
time: 925 us; the launch traced here: 923 us
  waiting for transfers between devices  633 us (68%)
  blocking collectives  122 us (13%)
  local copies, waits for them, and re-layouts  94.2 us (10%)
  matrix products  50.3 us (5%)
  between operations  14.5 us (2%)
    unnamed x10, waiting for transfers between devices  380 us
    all_gather x6, waiting for transfers between devices, collect(): lax.all_gather(for_sending(flats), ('clip', 'frame'), axis=0, tiled=True)  225 us
    unnamed x2, blocking collectives  84.4 us
    reshape x12, local copies, waits for them, and re-layouts, unflatten(): flat.reshape((-1,) + shape[1:])  32.6 us
    unnamed x133, local copies, waits for them, and re-layouts  30.2 us
    reduce_scatter x1, waiting for transfers between devices, body(): lax.psum_scatter(key_terms, 'frame', scatter_dimension=0, tiled=True)  28.3 us
    reshape x10, local copies, waits for them, and re-layouts, flatten(): return tuple((item.reshape(-1) for item in items))  26.4 us
    all_gather x1, blocking collectives, body(): lax.all_gather(values, 'frame', axis=0, tiled=True)  19.1 us
  transfers between devices with their start and end apart: 9, of which 7 were waited for; matrix products, arithmetic and copies ran while one was open for 12% of the time, Pallas kernels for 0%

commit v1 on v0

--- a/solution.py
+++ b/solution.py
@@ -10,14 +10,6 @@
 EPS = 1e-05
 SQRT_HALF = 0.7071067811865476
 INV_ROOT = 0.3989422804014327
-
-
-def for_sending(array):
-
-    def short(part):
-        return part.astype(jnp.bfloat16) if part.dtype == jnp.float32 else part
-
-    return jax.tree.map(short, array)
 
 
 def normalize(rows):
@@ -51,30 +43,22 @@
     return jnp.einsum("to,io->ti", left, right, preferred_element_type=jnp.float32)
 
 
-def flatten(items):
-    return tuple((item.reshape(-1) for item in items))
-
-
-def unflatten(flats, shapes):
-    return tuple((flat.reshape((-1,) + shape[1:]) for flat, shape in zip(flats, shapes)))
-
-
-def collect(params):
-    shapes = [item.shape for item in params]
-    flats = flatten(params)
-    whole = jax.tree.map(
-        lambda part, own: part.astype(own.dtype),
-        lax.all_gather(for_sending(flats), ("clip", "frame"), axis=0, tiled=True),
-        flats,
-    )
-    return unflatten(whole, shapes)
-
-
-def spread(grads):
-    shapes = [item.shape for item in grads]
-    flats = flatten(grads)
-    owned = lax.psum_scatter(flats, ("clip", "frame"), scatter_dimension=0, tiled=True)
-    return unflatten(owned, shapes)
+AXES = ("clip", "frame")
+f32 = jnp.float32
+bf16 = jnp.bfloat16
+
+
+def as_columns(vectors, rows):
+    return jnp.concatenate([item.reshape(-1, rows).T for item in vectors], axis=1)
+
+
+def gather_rows(part):
+    return lax.all_gather(part, AXES, axis=0, tiled=True)
+
+
+def scatter_rows(part):
+    half = lax.psum_scatter(part, "clip", scatter_dimension=0, tiled=True)
+    return lax.psum_scatter(half, "frame", scatter_dimension=0, tiled=True)
 
 
 def body(
@@ -96,43 +80,48 @@
     outer_bias,
     upstream,
 ):
-    f32 = jnp.float32
-    bf16 = jnp.bfloat16
     scale = HEAD_DIM ** (-0.5)
-    params = (
+    own = query_weight.shape[0]
+    vectors = (
         first_gain,
         first_bias,
-        query_weight,
         query_bias,
-        key_weight,
-        value_weight,
         value_bias,
-        output_weight,
         output_bias,
         second_gain,
         second_bias,
-        inner_weight,
-        inner_bias,
-        outer_weight,
         outer_bias,
     )
-    (
-        pre_gain,
-        pre_shift,
-        query_mat,
-        query_add,
-        key_mat,
-        value_mat,
-        value_add,
-        proj_mat,
-        proj_add,
-        post_gain,
-        post_shift,
-        inner_mat,
-        inner_add,
-        outer_mat,
-        outer_add,
-    ) = collect(params)
+    small = as_columns(vectors + (inner_bias,), own)
+    spare = -small.shape[1] % 128
+    small = jnp.pad(small, ((0, 0), (0, spare)))
+    sizes = (
+        query_weight.shape[1],
+        key_weight.shape[1],
+        value_weight.shape[1],
+        output_weight.shape[1],
+        inner_weight.shape[1],
+        small.shape[1],
+    )
+    ends = []
+    for size in sizes:
+        ends.append((ends[-1] if ends else 0) + size)
+    wide = gather_rows(
+        jnp.concatenate(
+            [query_weight, key_weight, value_weight, output_weight, inner_weight, small], axis=1
+        )
+    )
+    wide, outer_weight = lax.optimization_barrier((wide, outer_weight))
+    outer_mat = gather_rows(outer_weight)
+    (query_mat, key_mat, value_mat, proj_mat, inner_mat, shared) = jnp.split(wide, ends[:-1], axis=1)
+    total = query_mat.shape[0]
+    (pre_gain, pre_shift, query_add, value_add, proj_add, post_gain, post_shift, outer_add) = [
+        shared[:, at] for at in range(8)
+    ]
+    per = inner_bias.shape[0] // own
+    inner_add = (
+        shared[:, 8 : 8 + per].reshape(total // own, own, per).transpose(0, 2, 1).reshape(-1)
+    )
     local = layer_input.shape[0]
     width = layer_input.shape[1]
     rows = layer_input.astype(f32)
@@ -141,10 +130,8 @@
     queries = ((matmul(first_hidden, query_mat) + query_add.astype(f32)) * scale).astype(bf16)
     keys = matmul(first_hidden, key_mat).astype(bf16)
     values = (matmul(first_hidden, value_mat) + value_add.astype(f32)).astype(bf16)
-    all_keys, all_values = (
-        lax.all_gather(keys, "frame", axis=0, tiled=True),
-        lax.all_gather(values, "frame", axis=0, tiled=True),
-    )
+    both = lax.all_gather(jnp.concatenate([keys, values], axis=1), "frame", axis=0, tiled=True)
+    all_keys, all_values = both[:, :width], both[:, width:]
     q_heads = queries.reshape(local, HEADS, HEAD_DIM)
     k_heads = all_keys.reshape(-1, HEADS, HEAD_DIM)
     v_heads = all_values.reshape(-1, HEADS, HEAD_DIM)
@@ -162,23 +149,6 @@
     inner = matmul(second_hidden, inner_mat) + inner_add.astype(f32)
     activated = jax.nn.gelu(inner, approximate=False).astype(bf16)
     layer_output = (middle + matmul(activated, outer_mat) + outer_add.astype(f32)).astype(bf16)
-    (
-        pre_gain,
-        pre_shift,
-        query_mat,
-        query_add,
-        key_mat,
-        value_mat,
-        value_add,
-        proj_mat,
-        proj_add,
-        post_gain,
-        post_shift,
-        inner_mat,
-        inner_add,
-        outer_mat,
-        outer_add,
-    ) = collect(params)
     grad_out = upstream.astype(f32)
     g_outer_w = left_product(activated, upstream)
     g_outer_b = jnp.sum(grad_out, axis=0)
@@ -213,10 +183,10 @@
     value_terms = jnp.einsum(
         "hqk,qhd->khd", again_probs, g_heads, preferred_element_type=f32
     ).reshape(-1, width)
-    grad_keys, grad_values = (
-        lax.psum_scatter(key_terms, "frame", scatter_dimension=0, tiled=True),
-        lax.psum_scatter(value_terms, "frame", scatter_dimension=0, tiled=True),
-    )
+    pair = lax.psum_scatter(
+        jnp.concatenate([key_terms, value_terms], axis=1), "frame", scatter_dimension=0, tiled=True
+    )
+    grad_keys, grad_values = pair[:, :width], pair[:, width:]
     query_round = grad_queries.astype(bf16)
     key_round = grad_keys.astype(bf16)
     value_round = grad_values.astype(bf16)
@@ -235,43 +205,62 @@
     input_grad = (
         grad_middle + norm_back(grad_first * pre_gain.astype(f32), first_norm, first_rstd)
     ).astype(bf16)
-    owned = spread(
-        (
+    small_grads = [
+        item.reshape(-1, 1)
+        for item in (
             g_first_g,
             g_first_b,
-            g_query_w,
             g_query_b,
-            g_key_w,
-            g_value_w,
             g_value_b,
-            g_proj_w,
             g_proj_b,
             g_second_g,
             g_second_b,
-            g_inner_w,
-            g_inner_b,
-            g_outer_w,
             g_outer_b,
         )
-    )
+    ]
+    small_grads.append(
+        g_inner_b.reshape(total // own, per, own).transpose(0, 2, 1).reshape(total, per)
+    )
+    small_grads = jnp.concatenate(small_grads, axis=1)
+    small_grads = jnp.pad(small_grads, ((0, 0), (0, -small_grads.shape[1] % 128)))
+    o_outer_w = scatter_rows(g_outer_w.astype(bf16)).astype(f32)
+    last = scatter_rows(
+        jnp.concatenate(
+            [g_query_w, g_key_w, g_value_w, g_proj_w, g_inner_w, small_grads], axis=1
+        ).astype(bf16)
+    ).astype(f32)
+    (o_query_w, o_key_w, o_value_w, o_proj_w, o_inner_w, o_small) = jnp.split(
+        last, ends[:-1], axis=1
+    )
+    (
+        o_first_g,
+        o_first_b,
+        o_query_b,
+        o_value_b,
+        o_proj_b,
+        o_second_g,
+        o_second_b,
+        o_outer_b,
+    ) = [o_small[:, at] for at in range(8)]
+    o_inner_b = o_small[:, 8 : 8 + per].T.reshape(-1)
     return (
         layer_output,
         input_grad,
-        owned[0],
-        owned[1],
-        owned[2],
-        owned[3],
-        owned[4],
-        owned[5],
-        owned[6],
-        owned[7],
-        owned[8],
-        owned[9],
-        owned[10],
-        owned[11],
-        owned[12],
-        owned[13],
-        owned[14],
+        o_first_g,
+        o_first_b,
+        o_query_w,
+        o_query_b,
+        o_key_w,
+        o_value_w,
+        o_value_b,
+        o_proj_w,
+        o_proj_b,
+        o_second_g,
+        o_second_b,
+        o_inner_w,
+        o_inner_b,
+        o_outer_w,
+        o_outer_b,
     )
 
 

time: 925 us -> 497 us (0.54)
  waiting for transfers between devices: 633 us -> 356 us
  blocking collectives: 122 us -> 0 us
  local copies, waits for them, and re-layouts: 94.2 us -> 47.8 us
  matrix products: 50.3 us -> 60.5 us
    unnamed x10 -> x9, waiting for transfers between devices: 380 us -> 28.3 us
    reduce_scatter x2 -> x4, waiting for transfers between devices: 28.3 us -> 167 us  [the longest x2 112 us: scatter_rows(): half = lax.psum_scatter(part, 'clip', scatter_dimension=0, tiled=True)]
    unnamed x2 -> x0, blocking collectives: 84.4 us -> none
    all_gather x6 -> x3, waiting for transfers between devices: 225 us -> 161 us  [the longest x2 130 us: gather_rows(): return lax.all_gather(part, AXES, axis=0, tiled=True)]
    reshape x22 -> x12, local copies, waits for them, and re-layouts: 59 us -> 9.18 us  [the longest x8 4.98 us: body(): item.reshape(-1, 1)]
    all_gather x2 -> x0, blocking collectives: 37.9 us -> none  [the longest x1 19.1 us: body(): lax.all_gather(values, 'frame', axis=0, tiled=True)]
    unnamed x133 -> x128, local copies, waits for them, and re-layouts: 30.2 us -> 16.2 us
  transfers between devices with their start and end apart: 9 -> 8, of which waited for: 7 -> 8; matrix products, arithmetic and copies ran while one was open for 12% -> 15% of each run, Pallas kernels for 0% -> 0%
where the time goes in v1:
time: 497 us; the launch traced here: 495 us
  waiting for transfers between devices  356 us (72%)
  matrix products  60.5 us (12%)
  local copies, waits for them, and re-layouts  47.8 us (10%)
  other arithmetic  15.2 us (3%)
  between operations  14.9 us (3%)
    all_gather x2, waiting for transfers between devices, gather_rows(): return lax.all_gather(part, AXES, axis=0, tiled=True)  130 us
    reduce_scatter x2, waiting for transfers between devices, scatter_rows(): half = lax.psum_scatter(part, 'clip', scatter_dimension=0, tiled=True)  112 us
    reduce_scatter x1, waiting for transfers between devices, body(): lax.psum_scatter(jnp.concatenate([key_terms, value_terms], axis=1), 'fram...  34.1 us
    all_gather x1, waiting for transfers between devices, body(): lax.all_gather(jnp.concatenate([keys, values], axis=1), 'frame', axis=0,...  31 us
    unnamed x9, waiting for transfers between devices  28.3 us
    dot_general x6, matrix products, right_product(): jnp.einsum('to,io->ti', left, right, preferred_element_type=jnp.float32)  20.8 us
    reduce_scatter x1, waiting for transfers between devices, scatter_rows(): return lax.psum_scatter(half, 'frame', scatter_dimension=0, tiled=True)  20.3 us
    dot_general x6, matrix products, matmul(): return jnp.dot(left, right, preferred_element_type=jnp.float32)  18.4 us
  transfers between devices with their start and end apart: 8, of which 8 were waited for; matrix products, arithmetic and copies ran while one was open for 15% of the time, Pallas kernels for 0%

profile of v1, /device:TPU:0, one launch (start us, length us, event | category | flops | bytes accessed | tf_op | source)
XLA Modules:
  0.0 495.3 jit_solution(14912746424034809589)
XLA Ops:
  7.2 0.8 constant_dynamic-update-slice_fusion.5
  8.8 0.8 concatenate.20
  12.0 0.9 constant_dynamic-update-slice_fusion.1
  13.8 1.0 convert_reduce_fusion
  14.8 1.1 fusion.57
  16.0 83.3 %all-gather.4.cloned.1.call-done = bf16[768,6272]{1,0:T(8,128)(2,1)} async-done(((bf16[24,6272]{1,0:T(8,128)(2,1)}), bf16[768,6272]{1,0:T(8,128)(2,1)}) %all-gather.4.cloned.1.call-update) | async-done | bytes 9633808 | tf_op jit(solution)/shard_map/all_gather | solution.py:56
  99.3 3.5 convert_reduce_fusion.1
  102.8 1.6 convolution_convert_fusion.8
  104.4 1.6 fusion.30
  107.9 1.0 slice.94
  108.9 1.7 fusion.29
  111.8 31.0 %all-gather.6.cloned.1.call-done = bf16[512,1536]{1,0:T(8,128)(2,1)} async-done(((bf16[128,1536]{1,0:T(8,128)(2,1)}), bf16[512,1536]{1,0:T(8,128)(2,1)}) %all-gather.6.cloned.1.call-update) | async-done | bytes 1572880 | tf_op jit(solution)/shard_map/all_gather | solution.py:133
  142.7 1.5 fusion.70
  144.2 1.2 copy.81
  145.4 1.2 copy.83
  146.6 1.8 fusion.73
  148.4 0.8 exponential_reduce_fusion
  150.5 1.7 fusion.74
  152.9 7.9 %fusion.12 = (bf16[128,3072]{1,0:T(8,128)(2,1)}, f32[128,3072]{1,0:T(8,128)}) fusion(f32[3072]{0:T(1024)S(1)} %copy-done.40, bf16[768,6272]{1,0:T(8,128)(2,1)} %all-gather.4.cloned.1.call-done, f32[128,768]{1,0:T(8,128)S(1)} %get-tuple-element.58, f32[768]{0:T(1024)S(1)} %copy-done.28, f32[768]{0:T(1024)S(1)} %get-tuple-element.23, ...), kind=kOutput, calls=%fused_computation.19 | convolution fusion | flops 630423552 | bytes 7490560 | tf_op jit(solution)/shard_map/dot_general | solution.py:35
  160.8 47.2 %all-gather.8.cloned.1.call-done = bf16[3072,768]{1,0:T(8,128)(2,1)} async-done(((bf16[96,768]{1,0:T(8,128)(2,1)}), bf16[3072,768]{1,0:T(8,128)(2,1)}) %all-gather.8.cloned.1.call-update) | async-done | bytes 4718608 | tf_op jit(solution)/shard_map/all_gather | solution.py:56
  208.0 5.3 %fusion.75 = (bf16[3072]{0:T(1024)(128)(2,1)}, bf16[128,3072]{1,0:T(8,128)(2,1)S(1)}) fusion(f32[128,3072]{1,0:T(8,128)} %get-tuple-element.60, bf16[3072,768]{1,0:T(8,128)(2,1)} %all-gather.8.cloned.1.call-done, bf16[128,768]{1,0:T(8,128)(2,1)} %param.33), kind=kOutput, calls=%fused_computation.149 | convolution fusion | flops 608302080 | bytes 7280640 | tf_op jit(solution)/shard_map/to,io->ti/dot_general | solution.py:43
  213.3 5.0 %multiply_reduce_fusion = (bf16[768]{0:T(1024)(128)(2,1)}, f32[128]{0:T(128)S(1)}, f32[128]{0:T(128)S(1)}, bf16[768]{0:T(1024)(128)(2,1)}, f32[128,768]{1,0:T(8,128)S(1)}) fusion(f32[128,768]{1,0:T(8,128)S(1)} %get-tuple-element.58, f32[128]{0:T(128)S(1)} %copy-done.55, f32[128]{0:T(128)S(1)} %copy-done.52, f32[768]{0:T(1024)S(1)} %get-tuple-element.23, ...), kind=kOutput, calls=%fused_computation.99 | convolution fusion | flops 604862720 | bytes 6299648 | tf_op jit(solution)/shard_map/to,io->ti/dot_general | solution.py:43
  219.9 2.5 convolution_convert_fusion.6
  222.4 1.7 copy.85
  224.1 1.1 fusion.58
  225.2 1.8 fusion.46
  227.0 1.3 multiply_convert_fusion
  229.4 2.0 pad_maximum_fusion
  231.6 1.1 copy-done.10
  232.6 3.6 convolution_convert_fusion
  237.0 0.8 copy-done.1
  241.1 1.5 convolution_convert_fusion.5
  242.7 1.6 copy.91
  244.9 1.2 reshape.240
  246.1 1.3 reshape.241
  247.4 1.2 reshape.242
  248.6 1.4 reshape.244
  250.0 1.4 copy.86
  251.4 1.5 reshape.245
  252.9 1.2 constant_dynamic-update-slice_fusion.9
  254.1 2.6 fusion.33
  256.7 34.1 %reduce-scatter.8.cloned.1.call-done = f32[128,1536]{0,1:T(8,128)} async-done(((f32[512,1536]{0,1:T(8,128)}), f32[128,1536]{0,1:T(8,128)}) %reduce-scatter.8.cloned.1.call-update) | async-done | bytes 786448 | tf_op jit(solution)/shard_map/reduce_scatter | solution.py:186
  290.7 2.6 convolution_convert_fusion.3
  293.3 1.6 copy.89
  294.9 2.6 convolution_convert_fusion.2
  297.5 2.4 copy.90
  299.9 2.1 convolution_add_fusion.1
  302.2 3.3 fusion.56
  305.7 1.3 concatenate.24
  307.0 0.9 copy.87
  307.9 1.1 constant_dynamic-update-slice_fusion.8
  309.6 1.2 constant_dynamic-update-slice_fusion.7
  310.8 1.1 constant_dynamic-update-slice_fusion.6
  312.3 3.7 fusion
  316.8 31.1 %reduce-scatter.12.cloned.1.call-done = bf16[384,768]{1,0:T(8,128)(2,1)} async-done(((bf16[3072,768]{1,0:T(8,128)(2,1)}), bf16[384,768]{1,0:T(8,128)(2,1)}) %reduce-scatter.12.cloned.1.call-update) | async-done | bytes 589840 | tf_op jit(solution)/shard_map/reduce_scatter | solution.py:60
  348.0 81.2 %reduce-scatter.10.cloned.1.call-done = bf16[96,6272]{1,0:T(8,128)(2,1)} async-done(((bf16[768,6272]{1,0:T(8,128)(2,1)}), bf16[96,6272]{1,0:T(8,128)(2,1)}) %reduce-scatter.10.cloned.1.call-update) | async-done | bytes 1204240 | tf_op jit(solution)/shard_map/reduce_scatter | solution.py:60
  429.3 3.9 fusion.28
  433.2 20.3 %reduce-scatter.14.cloned.1.call-done = bf16[96,768]{1,0:T(8,128)(2,1)} async-done(((bf16[384,768]{1,0:T(8,128)(2,1)}), bf16[96,768]{1,0:T(8,128)(2,1)}) %reduce-scatter.14.cloned.1.call-update) | async-done | bytes 147472 | tf_op jit(solution)/shard_map/reduce_scatter | solution.py:61
  453.4 1.6 convert_element_type.222
  455.1 0.9 fusion.55
  456.0 27.5 %reduce-scatter.16.cloned.1.call-done = bf16[24,6272]{1,0:T(8,128)(2,1)} async-done(((bf16[96,6272]{1,0:T(8,128)(2,1)}), bf16[24,6272]{1,0:T(8,128)(2,1)}) %reduce-scatter.16.cloned.1.call-update) | async-done | bytes 301072
  483.5 1.1 convert_element_type.220
  484.6 0.8 slice_reduce_fusion.1
  486.2 1.5 fusion.72
  (170 shorter events, 19.8 us)
Async XLA Ops:
  7.2 95.6 %copy-start.2 = (bf16[128,768]{1,0:T(8,128)(2,1)S(1)}, bf16[128,768]{1,0:T(8,128)(2,1)}, u32[]{:S(2)}) copy-start(bf16[128,768]{1,0:T(8,128)(2,1)} %param.17) | copy-start | bytes 589828
  7.2 92.1 %all-gather.4.cloned.1.call-start = ((), (), s32[]{:S(2)}) async-start(), calls=%async_computation.5 | async-start | bytes 9934848 | tf_op jit(solution)/shard_map/all_gather | solution.py:56
  13.0 0.7 copy-start.27
  13.7 129.0 %all-gather.6.cloned.1.call-start = ((), (), s32[]{:S(2)}) async-start(), calls=%async_computation.6 | async-start | bytes 1966080 | tf_op jit(solution)/shard_map/all_gather | solution.py:133
  14.8 94.1 %copy-start.35 = (f32[128]{0:T(128)}, f32[128]{0:T(128)S(1)}, u32[]{:S(2)}) copy-start(f32[128]{0:T(128)S(1)} %broadcast_multiply_fusion.5) | copy-start | bytes 1540
  15.9 93.0 %copy-start.46 = (f32[128]{0:T(128)}, f32[128]{0:T(128)S(1)}, u32[]{:S(2)}) copy-start(f32[128]{0:T(128)S(1)} %add_rsqrt_fusion.1) | copy-start | bytes 1540
  102.8 6.1 %copy-start.30 = (f32[768]{0:T(1024)}, f32[768]{0:T(1024)S(1)}, u32[]{:S(2)}) copy-start(f32[768]{0:T(1024)S(1)} %get-tuple-element.27) | copy-start | bytes 9220
  106.9 101.1 %all-gather.8.cloned.1.call-start = ((), (), s32[]{:S(2)}) async-start(), calls=%async_computation.7 | async-start | bytes 4866048 | tf_op jit(solution)/shard_map/all_gather | solution.py:56
  107.6 183.1 %reduce-scatter.8.cloned.1.call-start = ((), (), s32[]{:S(2)}) async-start(), calls=%async_computation.8 | async-start | bytes 3932160 | tf_op jit(solution)/shard_map/reduce_scatter | solution.py:186
  110.8 35.8 %copy-start.18 = (bf16[128,768]{0,1:T(8,128)(2,1)}, bf16[128,768]{0,1:T(8,128)(2,1)S(1)}, u32[]{:S(2)}) copy-start(bf16[128,768]{0,1:T(8,128)(2,1)S(1)} %copy.82) | copy-start | bytes 589828
  148.4 1.1 copy-start.6
  149.5 0.9 copy-start.3
  149.5 0.9 copy-start.33
  150.3 1.9 copy-start.14
  150.3 2.6 copy-start.28
  150.3 2.6 copy-start.40
  208.0 5.3 %copy-start.52 = (f32[128]{0:T(128)S(1)}, f32[128]{0:T(128)}, u32[]{:S(2)}) copy-start(f32[128]{0:T(128)} %copy-done.51) | copy-start | bytes 1540
  208.0 5.3 %copy-start.55 = (f32[128]{0:T(128)S(1)}, f32[128]{0:T(128)}, u32[]{:S(2)}) copy-start(f32[128]{0:T(128)} %copy-done.54) | copy-start | bytes 1540
  213.3 5.0 %copy-start.24 = (bf16[128,3072]{1,0:T(8,128)(2,1)}, bf16[128,3072]{1,0:T(8,128)(2,1)S(1)}, u32[]{:S(2)}) copy-start(bf16[128,3072]{1,0:T(8,128)(2,1)S(1)} %get-tuple-element.65) | copy-start | bytes 2359300
  213.3 5.0 %copy-start.22 = (bf16[128,768]{1,0:T(8,128)(2,1)S(1)}, bf16[128,768]{1,0:T(8,128)(2,1)}, u32[]{:S(2)}) copy-start(bf16[128,768]{1,0:T(8,128)(2,1)} %param.33) | copy-start | bytes 589828
  219.1 0.8 copy-start.8
  225.2 1.8 copy-start.7
  225.2 1.8 copy-start.13
  227.0 1.3 copy-start.19
  228.3 1.1 copy-start
  231.5 1.1 copy-start.10
  231.5 1.2 copy-start.23
  231.5 116.5 %reduce-scatter.12.cloned.1.call-start = ((), (), s32[]{:S(2)}) async-start(), calls=%async_computation.10 | async-start | bytes 5308416 | tf_op jit(solution)/shard_map/reduce_scatter | solution.py:60
  236.3 1.6 copy-start.1
  236.3 1.8 copy-start.5
  236.3 3.2 copy-start.4
  236.3 3.2 copy-start.31
  236.3 3.2 copy-start.36
  236.3 3.2 copy-start.47
  236.3 192.9 %reduce-scatter.10.cloned.1.call-start = ((), (), s32[]{:S(2)}) async-start(), calls=%async_computation.9 | async-start | bytes 10838016 | tf_op jit(solution)/shard_map/reduce_scatter | solution.py:60
  240.1 1.0 copy-start.9
  240.1 1.0 copy-start.15
  244.2 9.8 %copy-start.21 = (bf16[128,12,64]{0,2,1:T(8,128)(2,1)S(1)}, bf16[128,12,64]{0,2,1:T(8,128)(2,1)}, u32[]{:S(2)}) copy-start(bf16[128,12,64]{0,2,1:T(8,128)(2,1)} %copy-done.20) | copy-start | bytes 589828
  252.9 37.9 %copy-start.37 = (f32[128]{0:T(128)S(1)}, f32[128]{0:T(128)}, u32[]{:S(2)}) copy-start(f32[128]{0:T(128)} %copy-done.35) | copy-start | bytes 1540
  254.1 36.7 %copy-start.48 = (f32[128]{0:T(128)S(1)}, f32[128]{0:T(128)}, u32[]{:S(2)}) copy-start(f32[128]{0:T(128)} %copy-done.46) | copy-start | bytes 1540
  293.3 1.6 copy-start.49
  299.9 2.2 copy-start.16
  299.9 2.2 copy-start.38
  302.1 3.6 copy-start.32
  302.1 3.6 copy-start.41
  302.1 3.5 copy-start.42
  302.1 3.5 copy-start.43
  302.2 3.5 copy-start.44
  302.2 3.5 copy-start.45
  307.9 1.7 copy-start.12
  310.8 1.5 copy-start.25
  310.8 1.5 copy-start.29
  310.8 1.5 copy-start.53
  310.8 1.5 copy-start.56
  316.8 112.5 %copy-start.11 = (bf16[128,3072]{1,0:T(8,128)(2,1)S(1)}, bf16[128,3072]{1,0:T(8,128)(2,1)}, u32[]{:S(2)}) copy-start(bf16[128,3072]{1,0:T(8,128)(2,1)} %get-tuple-element.59) | copy-start | bytes 2359300
  316.8 112.5 %copy-start.34 = (f32[768]{0:T(1024)S(1)}, f32[768]{0:T(1024)}, u32[]{:S(2)}) copy-start(f32[768]{0:T(1024)} %get-tuple-element.21) | copy-start | bytes 9220
  316.8 136.7 %reduce-scatter.14.cloned.1.call-start = ((), (), s32[]{:S(2)}) async-start(), calls=%async_computation.11 | async-start | bytes 737280 | tf_op jit(solution)/shard_map/reduce_scatter | solution.py:61
  348.0 135.5 %reduce-scatter.16.cloned.1.call-start = ((), (), s32[]{:S(2)}) async-start(), calls=%async_computation.12 | async-start | bytes 1505280
  429.3 25.8 %copy-start.58 = (f32[128]{0:T(128)S(1)}, f32[128]{0:T(128)}, u32[]{:S(2)}) copy-start(f32[128]{0:T(128)} %get-tuple-element.40) | copy-start | bytes 1540
  429.3 25.8 %copy-start.57 = (f32[128]{0:T(128)S(1)}, f32[128]{0:T(128)}, u32[]{:S(2)}) copy-start(f32[128]{0:T(128)} %get-tuple-element.41) | copy-start | bytes 1540
  429.3 25.8 %copy-start.26 = (f32[128,768]{1,0:T(8,128)S(1)}, f32[128,768]{1,0:T(8,128)}, u32[]{:S(2)}) copy-start(f32[128,768]{1,0:T(8,128)} %get-tuple-element.63) | copy-start | bytes 1179652
  429.3 25.8 %copy-start.39 = (f32[128]{0:T(128)S(1)}, f32[128]{0:T(128)}, u32[]{:S(2)}) copy-start(f32[128]{0:T(128)} %copy-done.35) | copy-start | bytes 1540
  429.3 25.8 %copy-start.50 = (f32[128]{0:T(128)S(1)}, f32[128]{0:T(128)}, u32[]{:S(2)}) copy-start(f32[128]{0:T(128)} %copy-done.46) | copy-start | bytes 1540
  483.5 4.2 copy-start.17
  (3 other events, 1.7 us)
Sparse Core Ops, SparseCore 0:
  13.8 85.3 all-gather.3
  107.0 35.6 all-gather.5
  145.5 62.4 all-gather.7
  231.6 59.0 reduce-scatter.7
  294.0 53.8 reduce-scatter.11
  351.8 77.4 reduce-scatter.9
  431.5 21.8 reduce-scatter.13
  455.8 27.7 reduce-scatter.15

commit v2 on v1

--- a/solution.py
+++ b/solution.py
@@ -1,6 +1,10 @@
+import functools
+
 import jax
 import jax.numpy as jnp
 from jax import lax
+from jax.experimental import pallas as pl
+from jax.experimental.pallas import tpu as pltpu
 from jax.sharding import PartitionSpec as P
 
 HEADS = 12
@@ -56,9 +60,108 @@
     return lax.all_gather(part, AXES, axis=0, tiled=True)
 
 
-def scatter_rows(part):
-    half = lax.psum_scatter(part, "clip", scatter_dimension=0, tiled=True)
-    return lax.psum_scatter(half, "frame", scatter_dimension=0, tiled=True)
+def reversed_bits(value, bits):
+    total = 0
+    for at in range(bits):
+        total = total + ((value // 2**at) % 2) * 2 ** (bits - 1 - at)
+    return total
+
+
+def halving_steps(clip, frame, clip_bits, frame_bits):
+    core = clip % 2
+    steps = [(core, clip + 1 - 2 * core, frame)]
+    for step in range(1, clip_bits):
+        down, up = 2 ** (clip_bits - step), 2**step
+        bit = ((clip // down) % 2) * (1 - core) + ((clip // up) % 2) * core
+        stride = down * (1 - core) + up * core
+        steps.append((bit, clip + (1 - 2 * bit) * stride, frame))
+    for step in range(frame_bits):
+        bit = (frame // 2**step) % 2
+        steps.append((bit, clip, frame + (1 - 2 * bit) * 2**step))
+    return steps
+
+
+def greet(steps):
+    barrier = pltpu.get_barrier_semaphore()
+    for _, clip, frame in steps:
+        pl.semaphore_signal(
+            barrier, inc=1, device_id=(clip, frame), device_id_type=pl.DeviceIdType.MESH
+        )
+    pl.semaphore_wait(barrier, len(steps))
+
+
+def scatter_kernel(clip_bits, frame_bits, terms, out, *scratch):
+    count = clip_bits + frame_bits
+    current, arrived = scratch[0], scratch[1 : 1 + count]
+    send_sems, recv_sems = scratch[1 + count], scratch[2 + count]
+    clip, frame = lax.axis_index("clip"), lax.axis_index("frame")
+    steps = halving_steps(clip, frame, clip_bits, frame_bits)
+    greet(steps)
+    core = steps[0][0]
+    frames = 2**frame_bits
+
+    def push(step, source):
+        copy = pltpu.make_async_remote_copy(
+            src_ref=source,
+            dst_ref=arrived[step],
+            send_sem=send_sems.at[step],
+            recv_sem=recv_sems.at[step],
+            device_id=(steps[step][1], steps[step][2]),
+            device_id_type=pl.DeviceIdType.MESH,
+        )
+        copy.start()
+        copy.wait()
+
+    push(0, terms.at[:, 1 - core])
+
+    def first_sum(at, carry):
+        group, lane = at // frames, at % frames
+        slot = group * (1 - core) + reversed_bits(group, clip_bits - 1) * core
+        slot = slot * frames + reversed_bits(lane, frame_bits)
+        current[slot] = (
+            terms[group, core, lane].astype(f32) + arrived[0][group, lane].astype(f32)
+        ).astype(bf16)
+        return carry
+
+    lax.fori_loop(0, current.shape[0], first_sum, 0)
+    held = current
+    for step in range(1, count):
+        bit = steps[step][0]
+        half = held.shape[0] // 2
+        push(step, held.at[pl.ds((1 - bit) * half, half)])
+        if step == count - 1:
+            out[...] = held[bit].astype(f32) + arrived[step][0].astype(f32)
+            break
+
+        def next_sum(at, carry, held=held, step=step, bit=bit, half=half):
+            arrived[step][at] = (
+                held[bit * half + at].astype(f32) + arrived[step][at].astype(f32)
+            ).astype(bf16)
+            return carry
+
+        lax.fori_loop(0, half, next_sum, 0)
+        held = arrived[step]
+
+
+def scatter_blocks(blocks, clips, frames):
+    count, rows, columns = blocks.shape
+    clip_bits, frame_bits = clips.bit_length() - 1, frames.bit_length() - 1
+    steps = clip_bits + frame_bits
+    arrivals = [pltpu.VMEM((clips // 2, frames, rows, columns), bf16)]
+    for step in range(1, steps):
+        arrivals.append(pltpu.VMEM((count >> (step + 1), rows, columns), bf16))
+    return pl.pallas_call(
+        functools.partial(scatter_kernel, clip_bits, frame_bits),
+        out_shape=jax.ShapeDtypeStruct((rows, columns), f32),
+        in_specs=[pl.BlockSpec(memory_space=pltpu.VMEM)],
+        out_specs=pl.BlockSpec(memory_space=pltpu.VMEM),
+        scratch_shapes=[pltpu.VMEM((count // 2, rows, columns), bf16)]
+        + arrivals
+        + [pltpu.SemaphoreType.DMA((steps,)), pltpu.SemaphoreType.DMA((steps,))],
+        compiler_params=pltpu.CompilerParams(
+            collective_id=1, has_side_effects=True, vmem_limit_bytes=52 * 2**20
+        ),
+    )(blocks.reshape(clips // 2, 2, frames, rows, columns))
 
 
 def body(
@@ -184,8 +287,9 @@
         "hqk,qhd->khd", again_probs, g_heads, preferred_element_type=f32
     ).reshape(-1, width)
     pair = lax.psum_scatter(
-        jnp.concatenate([key_terms, value_terms], axis=1), "frame", scatter_dimension=0, tiled=True
-    )
+        jnp.concatenate([key_terms, value_terms], axis=1).astype(bf16), "frame", scatter_dimension=0, tiled=True
+    )
+    pair = pair.astype(f32)
     grad_keys, grad_values = pair[:, :width], pair[:, width:]
     query_round = grad_queries.astype(bf16)
     key_round = grad_keys.astype(bf16)
@@ -221,17 +325,30 @@
     small_grads.append(
         g_inner_b.reshape(total // own, per, own).transpose(0, 2, 1).reshape(total, per)
     )
+    devices = total // own
     small_grads = jnp.concatenate(small_grads, axis=1)
-    small_grads = jnp.pad(small_grads, ((0, 0), (0, -small_grads.shape[1] % 128)))
-    o_outer_w = scatter_rows(g_outer_w.astype(bf16)).astype(f32)
-    last = scatter_rows(
-        jnp.concatenate(
-            [g_query_w, g_key_w, g_value_w, g_proj_w, g_inner_w, small_grads], axis=1
-        ).astype(bf16)
-    ).astype(f32)
-    (o_query_w, o_key_w, o_value_w, o_proj_w, o_inner_w, o_small) = jnp.split(
-        last, ends[:-1], axis=1
-    )
+    kinds = small_grads.shape[1]
+    small_rows = small_grads.reshape(devices, own, kinds).transpose(0, 2, 1).reshape(devices, -1)
+    used = 4 * own + g_inner_w.shape[1] // width * own + g_outer_w.shape[0] // devices
+    tail = -(-small_rows.shape[1] // width)
+    tail += -(used + tail) % 16
+    small_rows = jnp.pad(small_rows, ((0, 0), (0, tail * width - small_rows.shape[1])))
+    pieces = [g_query_w, g_key_w, g_value_w, g_proj_w]
+    pieces += [g_inner_w[:, at : at + width] for at in range(0, g_inner_w.shape[1], width)]
+    pieces += [g_outer_w, small_rows.reshape(devices * tail, width)]
+    blocks = jnp.concatenate(
+        [item.reshape(devices, -1, width).astype(bf16) for item in pieces], axis=1
+    )
+    mine = scatter_blocks(blocks, lax.axis_size("clip"), lax.axis_size("frame"))
+    (o_query_w, o_key_w, o_value_w, o_proj_w) = [
+        mine[at * own : (at + 1) * own] for at in range(4)
+    ]
+    o_inner_w = jnp.concatenate(
+        [mine[at * own : (at + 1) * own] for at in range(4, 4 + g_inner_w.shape[1] // width)],
+        axis=1,
+    )
+    o_outer_w = mine[used - g_outer_w.shape[0] // devices : used]
+    o_small = mine[used:].reshape(-1)[: kinds * own].reshape(kinds, own)
     (
         o_first_g,
         o_first_b,
@@ -241,8 +358,8 @@
         o_second_g,
         o_second_b,
         o_outer_b,
-    ) = [o_small[:, at] for at in range(8)]
-    o_inner_b = o_small[:, 8 : 8 + per].T.reshape(-1)
+    ) = [o_small[at] for at in range(8)]
+    o_inner_b = o_small[8:].reshape(-1)
     return (
         layer_output,
         input_grad,

time: 497 us -> 431 us (0.87)
  waiting for transfers between devices: 356 us -> 182 us
  Pallas kernels: 0 us -> 129 us
  matrix products: 60.5 us -> 49.5 us
  local copies, waits for them, and re-layouts: 47.8 us -> 42.4 us
    reduce_scatter x4 -> x0, waiting for transfers between devices: 167 us -> none  [the longest x2 112 us: scatter_rows(): half = lax.psum_scatter(part, 'clip', scatter_dimension=0, tiled=True)]
    pallas_call x0 -> x1, Pallas kernels: none -> 129 us  [scatter_blocks(): pl.pallas_call(functools.partial(scatter_kernel, clip_bits, frame_bits),...]
    unnamed x9 -> x5, waiting for transfers between devices: 28.3 us -> 21.8 us
    dot_general x6, matrix products: 14.6 us -> 8.17 us  [left_product(): jnp.einsum('ti,to->io', left, right, preferred_element_type=jnp.float32)]
    another operation x4 -> x0, local copies, waits for them, and re-layouts: 6.19 us -> none
    reshape x9 -> x1, local copies, waits for them, and re-layouts: 5.58 us -> 0.01 us  [body(): o_small = mine[used:].reshape(-1)[:kinds * own].reshape(kinds, own)]
  transfers between devices with their start and end apart: 8 -> 4, of which waited for: 8 -> 4; matrix products, arithmetic and copies ran while one was open for 15% -> 8% of each run, Pallas kernels for 0% -> 0%
where the time goes in v2:
time: 431 us; the launch traced here: 430 us
  waiting for transfers between devices  182 us (42%)
  Pallas kernels  129 us (30%)
  matrix products  49.5 us (11%)
  local copies, waits for them, and re-layouts  42.4 us (10%)
  between operations  14.6 us (3%)
  other arithmetic  12.2 us (3%)
    all_gather x2, waiting for transfers between devices, gather_rows(): return lax.all_gather(part, AXES, axis=0, tiled=True)  130 us
    pallas_call x1, Pallas kernels, scatter_blocks(): pl.pallas_call(functools.partial(scatter_kernel, clip_bits, frame_bits),...  129 us
    all_gather x1, waiting for transfers between devices, body(): lax.all_gather(jnp.concatenate([keys, values], axis=1), 'frame', axis=0,...  30.3 us
    unnamed x5, waiting for transfers between devices  21.8 us
    unnamed x128, local copies, waits for them, and re-layouts  20.9 us
    dot_general x6, matrix products, right_product(): jnp.einsum('to,io->ti', left, right, preferred_element_type=jnp.float32)  18.4 us
    dot_general x6, matrix products, matmul(): return jnp.dot(left, right, preferred_element_type=jnp.float32)  16.1 us
  transfers between devices with their start and end apart: 4, of which 4 were waited for; matrix products, arithmetic and copies ran while one was open for 8% of the time, Pallas kernels for 0%

profile of v2, /device:TPU:0, one launch (start us, length us, event | category | flops | bytes accessed | tf_op | source)
XLA Modules:
  0.0 430.3 jit_solution(6749729551027517325)
XLA Ops:
  7.2 0.8 constant_dynamic-update-slice_fusion.5
  8.1 0.7 reshape.278
  8.8 0.8 concatenate.40
  9.7 0.8 constant_dynamic-update-slice_fusion.4
  10.5 0.8 constant_dynamic-update-slice_fusion.3
  11.3 0.8 constant_dynamic-update-slice_fusion.2
  12.0 0.9 constant_dynamic-update-slice_fusion.1
  13.8 1.0 convert_reduce_fusion
  14.8 1.1 fusion.57
  16.0 83.3 %all-gather.4.cloned.1.call-done = bf16[768,6272]{1,0:T(8,128)(2,1)} async-done(((bf16[24,6272]{1,0:T(8,128)(2,1)}), bf16[768,6272]{1,0:T(8,128)(2,1)}) %all-gather.4.cloned.1.call-update) | async-done | bytes 9633808 | tf_op jit(solution)/shard_map/all_gather | solution.py:60
  99.3 3.7 convert_reduce_fusion.1
  103.0 1.6 convolution_convert_fusion.10
  104.6 1.6 fusion.31
  106.3 0.8 pad_maximum_fusion.1
  108.0 1.0 slice.153
  109.1 1.7 fusion.30
  110.8 0.8 copy.65
  111.9 0.7 reshape.296
  112.6 30.3 %all-gather.6.cloned.1.call-done = bf16[512,1536]{1,0:T(8,128)(2,1)} async-done(((bf16[128,1536]{1,0:T(8,128)(2,1)}), bf16[512,1536]{1,0:T(8,128)(2,1)}) %all-gather.6.cloned.1.call-update) | async-done | bytes 1572880 | tf_op jit(solution)/shard_map/all_gather | solution.py:236
  142.9 1.5 fusion.76
  144.4 1.2 copy.64
  145.6 1.2 copy.66
  146.8 1.9 fusion.80
  148.7 0.8 exponential_reduce_fusion
  149.9 0.8 convolution_convert_fusion.9
  150.8 1.7 fusion.81
  153.3 7.9 %fusion.11 = (bf16[128,3072]{1,0:T(8,128)(2,1)}, f32[128,3072]{1,0:T(8,128)}) fusion(f32[3072]{0:T(1024)S(1)} %copy-done.38, bf16[768,6272]{1,0:T(8,128)(2,1)} %all-gather.4.cloned.1.call-done, f32[128,768]{1,0:T(8,128)S(1)} %get-tuple-element.67, f32[768]{0:T(1024)S(1)} %copy-done.30, f32[768]{0:T(1024)S(1)} %get-tuple-element.23, ...), kind=kOutput, calls=%fused_computation.17 | convolution fusion | flops 630423552 | bytes 7490560 | tf_op jit(solution)/shard_map/dot_general | solution.py:39
  161.2 47.0 %all-gather.8.cloned.1.call-done = bf16[3072,768]{1,0:T(8,128)(2,1)} async-done(((bf16[96,768]{1,0:T(8,128)(2,1)}), bf16[3072,768]{1,0:T(8,128)(2,1)}) %all-gather.8.cloned.1.call-update) | async-done | bytes 4718608 | tf_op jit(solution)/shard_map/all_gather | solution.py:60
  208.2 5.3 %fusion.82 = (bf16[3072]{0:T(1024)(128)(2,1)}, bf16[128,3072]{1,0:T(8,128)(2,1)S(1)}) fusion(f32[128,3072]{1,0:T(8,128)} %get-tuple-element.69, bf16[3072,768]{1,0:T(8,128)(2,1)} %all-gather.8.cloned.1.call-done, bf16[128,768]{1,0:T(8,128)(2,1)} %param.33), kind=kOutput, calls=%fused_computation.152 | convolution fusion | flops 608302080 | bytes 7280640 | tf_op jit(solution)/shard_map/to,io->ti/dot_general | solution.py:47
  213.5 5.0 %multiply_reduce_fusion = (bf16[768]{0:T(1024)(128)(2,1)}, f32[128]{0:T(128)S(1)}, f32[128]{0:T(128)S(1)}, bf16[768]{0:T(1024)(128)(2,1)}, f32[128,768]{1,0:T(8,128)S(1)}) fusion(f32[128,768]{1,0:T(8,128)S(1)} %get-tuple-element.67, f32[128]{0:T(128)S(1)} %copy-done.47, f32[128]{0:T(128)S(1)} %copy-done.42, f32[768]{0:T(1024)S(1)} %get-tuple-element.23, ...), kind=kOutput, calls=%fused_computation.100 | convolution fusion | flops 604862720 | bytes 6299648 | tf_op jit(solution)/shard_map/to,io->ti/dot_general | solution.py:47
  218.5 0.8 fusion.74
  219.3 0.8 copy-done.9
  220.1 2.5 convolution_convert_fusion.8
  222.6 1.7 copy.68
  224.3 1.1 fusion.58
  225.4 1.8 convolution_convert_fusion.6
  227.2 1.3 multiply_convert_fusion
  228.5 1.1 copy-done.1
  230.1 1.6 copy.91
  231.7 0.9 copy-done.26
  233.0 3.5 convolution_convert_fusion
  236.5 0.7 fusion.78
  237.8 1.8 fusion.34
  239.7 1.5 convolution_convert_fusion.1
  241.2 2.3 fusion.75
  243.5 1.5 fusion.29
  245.0 21.0 %reduce-scatter.4.cloned.1.call-done = bf16[128,1536]{1,0:T(8,128)(2,1)} async-done(((bf16[512,1536]{1,0:T(8,128)(2,1)}), bf16[128,1536]{1,0:T(8,128)(2,1)}) %reduce-scatter.4.cloned.1.call-update) | async-done | bytes 393232
  266.0 1.9 convolution_add_fusion.1
  268.0 1.9 convolution_add_fusion
  270.0 0.7 copy-done.16
  270.7 0.8 fusion.56
  271.5 0.8 copy.69
  273.0 0.8 copy.79
  273.7 1.3 pad.10
  275.1 2.5 copy.80
  277.6 1.5 fusion.24
  281.2 0.9 copy-done.15
  282.7 0.9 copy-done.13
  284.5 0.8 copy-done.21
  285.3 5.3 %copy-done = bf16[32,304,768]{2,1,0:T(8,128)(2,1)} copy-done((bf16[32,304,768]{2,1,0:T(8,128)(2,1)}, bf16[32,304,768]{2,1,0:T(8,128)(2,1)S(1)}, u32[]{:S(2)}) %copy-start) | copy-done | bytes 14942232
  290.6 128.8 %shard_map.296 = f32[304,768]{1,0:T(8,128)S(1)} custom-call(bf16[4,2,4,304,768]{4,3,2,1,0:T(8,128)(2,1)} %bitcast.90), custom_call_target="tpu_custom_call" | custom-call | tf_op jit(solution)/shard_map/pallas_call | solution.py:153
  421.4 0.7 slice.179
  422.2 0.9 fusion.55
  423.1 0.7 pad_maximum_fusion.2
  (159 shorter events, 10.7 us)
Async XLA Ops:
  7.2 95.8 %copy-start.3 = (bf16[128,768]{1,0:T(8,128)(2,1)S(1)}, bf16[128,768]{1,0:T(8,128)(2,1)}, u32[]{:S(2)}) copy-start(bf16[128,768]{1,0:T(8,128)(2,1)} %param.17) | copy-start | bytes 589828
  7.2 92.1 %all-gather.4.cloned.1.call-start = ((), (), s32[]{:S(2)}) async-start(), calls=%async_computation.1 | async-start | bytes 9934848 | tf_op jit(solution)/shard_map/all_gather | solution.py:60
  13.0 0.7 copy-start.29
  13.7 129.2 %all-gather.6.cloned.1.call-start = ((), (), s32[]{:S(2)}) async-start(), calls=%async_computation.2 | async-start | bytes 1966080 | tf_op jit(solution)/shard_map/all_gather | solution.py:236
  14.8 94.3 %copy-start.36 = (f32[128]{0:T(128)}, f32[128]{0:T(128)S(1)}, u32[]{:S(2)}) copy-start(f32[128]{0:T(128)S(1)} %broadcast_multiply_fusion.5) | copy-start | bytes 1540
  15.9 93.2 %copy-start.39 = (f32[128]{0:T(128)}, f32[128]{0:T(128)S(1)}, u32[]{:S(2)}) copy-start(f32[128]{0:T(128)S(1)} %add_rsqrt_fusion.1) | copy-start | bytes 1540
  103.0 6.2 %copy-start.32 = (f32[768]{0:T(1024)}, f32[768]{0:T(1024)S(1)}, u32[]{:S(2)}) copy-start(f32[768]{0:T(1024)S(1)} %get-tuple-element.27) | copy-start | bytes 9220
  107.1 101.1 %all-gather.8.cloned.1.call-start = ((), (), s32[]{:S(2)}) async-start(), calls=%async_computation.3 | async-start | bytes 4866048 | tf_op jit(solution)/shard_map/all_gather | solution.py:60
  107.8 158.2 %reduce-scatter.4.cloned.1.call-start = ((), (), s32[]{:S(2)}) async-start(), calls=%async_computation.4 | async-start | bytes 1966080
  148.7 1.1 copy-start.7
  149.9 0.9 copy-start.4
  149.9 0.9 copy-start.34
  150.7 1.9 copy-start.19
  150.7 2.6 copy-start.30
  150.7 2.6 copy-start.38
  152.5 0.5 copy-start.41
  152.7 0.5 copy-start.46
  208.2 5.3 %copy-start.42 = (f32[128]{0:T(128)S(1)}, f32[128]{0:T(128)}, u32[]{:S(2)}) copy-start(f32[128]{0:T(128)} %copy-done.41) | copy-start | bytes 1540
  208.2 5.3 %copy-start.47 = (f32[128]{0:T(128)S(1)}, f32[128]{0:T(128)}, u32[]{:S(2)}) copy-start(f32[128]{0:T(128)} %copy-done.46) | copy-start | bytes 1540
  213.5 5.0 %copy-start.27 = (bf16[128,3072]{1,0:T(8,128)(2,1)}, bf16[128,3072]{1,0:T(8,128)(2,1)S(1)}, u32[]{:S(2)}) copy-start(bf16[128,3072]{1,0:T(8,128)(2,1)S(1)} %get-tuple-element.73) | copy-start | bytes 2359300
  213.5 5.0 %copy-start.25 = (bf16[128,768]{1,0:T(8,128)(2,1)S(1)}, bf16[128,768]{1,0:T(8,128)(2,1)}, u32[]{:S(2)}) copy-start(bf16[128,768]{1,0:T(8,128)(2,1)} %param.33) | copy-start | bytes 589828
  219.3 0.8 copy-start.9
  225.4 1.8 copy-start.8
  225.4 1.8 copy-start.18
  227.2 2.4 copy-start.24
  228.5 1.2 copy-start.1
  231.7 0.9 copy-start.26
  231.7 1.2 copy-start.11
  233.0 3.5 copy-start.2
  233.0 3.5 copy-start.6
  236.5 0.9 copy-start.44
  236.5 1.0 copy-start.50
  236.5 1.1 copy-start.49
  236.5 1.2 copy-start.45
  237.3 2.4 copy-start.28
  237.3 2.4 copy-start.31
  237.3 2.4 copy-start.43
  237.3 2.4 copy-start.48
  239.7 3.8 slice-start.2
  241.2 2.3 slice-start.3
  241.2 2.3 copy-start.35
  266.0 2.0 copy-start.22
  268.0 2.7 copy-start.5
  268.0 2.7 copy-start.33
  268.0 2.7 copy-start.37
  268.0 2.7 copy-start.40
  269.9 0.8 copy-start.16
  277.6 1.5 copy-start.23
  279.7 1.0 copy-start.10
  279.7 1.0 copy-start.20
  279.8 4.3 slice-start
  280.4 1.7 copy-start.15
  281.2 1.4 copy-start.14
  282.1 2.0 slice-start.1
  282.2 1.4 copy-start.13
  282.7 1.4 copy-start.12
  284.1 1.1 copy-start.21
  285.3 5.3 %copy-start = (bf16[32,304,768]{2,1,0:T(8,128)(2,1)}, bf16[32,304,768]{2,1,0:T(8,128)(2,1)S(1)}, u32[]{:S(2)}) copy-start(bf16[32,304,768]{2,1,0:T(8,128)(2,1)S(1)} %constant_dynamic-update-slice_fusion.6) | copy-start | bytes 44826628
  419.5 2.7 copy-start.52
  419.5 2.7 copy-start.51
  419.5 2.7 copy-start.17
Sparse Core Ops, SparseCore 0:
  13.8 85.3 all-gather.3
  107.2 35.6 all-gather.5
  145.7 62.4 all-gather.7
  231.9 34.1 reduce-scatter.3

commit v3 on v2

--- a/solution.py
+++ b/solution.py
@@ -90,7 +90,7 @@
     pl.semaphore_wait(barrier, len(steps))
 
 
-def scatter_kernel(clip_bits, frame_bits, terms, out, *scratch):
+def scatter_kernel(clip_bits, frame_bits, chunks, terms, out, *scratch):
     count = clip_bits + frame_bits
     current, arrived = scratch[0], scratch[1 : 1 + count]
     send_sems, recv_sems = scratch[1 + count], scratch[2 + count]
@@ -100,64 +100,81 @@
     core = steps[0][0]
     frames = 2**frame_bits
 
-    def push(step, source):
+    def push(step, chunk, source):
+        rows = pl.ds(*chunks[chunk])
+        target = arrived[step].at[:, :, rows] if step == 0 else arrived[step].at[:, rows]
         copy = pltpu.make_async_remote_copy(
             src_ref=source,
-            dst_ref=arrived[step],
-            send_sem=send_sems.at[step],
-            recv_sem=recv_sems.at[step],
+            dst_ref=target,
+            send_sem=send_sems.at[step, chunk],
+            recv_sem=recv_sems.at[step, chunk],
             device_id=(steps[step][1], steps[step][2]),
             device_id_type=pl.DeviceIdType.MESH,
         )
         copy.start()
-        copy.wait()
-
-    push(0, terms.at[:, 1 - core])
-
-    def first_sum(at, carry):
-        group, lane = at // frames, at % frames
-        slot = group * (1 - core) + reversed_bits(group, clip_bits - 1) * core
-        slot = slot * frames + reversed_bits(lane, frame_bits)
-        current[slot] = (
-            terms[group, core, lane].astype(f32) + arrived[0][group, lane].astype(f32)
-        ).astype(bf16)
-        return carry
-
-    lax.fori_loop(0, current.shape[0], first_sum, 0)
+        return copy
+
+    flying = [
+        push(0, chunk, terms.at[:, 1 - core, :, pl.ds(*chunks[chunk])])
+        for chunk in range(len(chunks))
+    ]
     held = current
-    for step in range(1, count):
-        bit = steps[step][0]
-        half = held.shape[0] // 2
-        push(step, held.at[pl.ds((1 - bit) * half, half)])
-        if step == count - 1:
-            out[...] = held[bit].astype(f32) + arrived[step][0].astype(f32)
-            break
-
-        def next_sum(at, carry, held=held, step=step, bit=bit, half=half):
-            arrived[step][at] = (
-                held[bit * half + at].astype(f32) + arrived[step][at].astype(f32)
-            ).astype(bf16)
-            return carry
-
-        lax.fori_loop(0, half, next_sum, 0)
-        held = arrived[step]
+    for step in range(count):
+        for chunk, (first, size) in enumerate(chunks):
+            rows = pl.ds(first, size)
+            flying[chunk].wait()
+            if step == 0:
+
+                def first_sum(at, carry, rows=rows):
+                    group, lane = at // frames, at % frames
+                    slot = group * (1 - core) + reversed_bits(group, clip_bits - 1) * core
+                    slot = slot * frames + reversed_bits(lane, frame_bits)
+                    current[slot, rows] = (
+                        terms[group, core, lane, rows].astype(f32)
+                        + arrived[0][group, lane, rows].astype(f32)
+                    ).astype(bf16)
+                    return carry
+
+                lax.fori_loop(0, current.shape[0], first_sum, 0)
+                after = current
+            else:
+                bit, half, after = steps[step][0], held.shape[0] // 2, arrived[step]
+                if step == count - 1:
+                    out[rows] = held[bit, rows].astype(f32) + after[0, rows].astype(f32)
+                    continue
+
+                def next_sum(at, carry, rows=rows, held=held, after=after, bit=bit, half=half):
+                    after[at, rows] = (
+                        held[bit * half + at, rows].astype(f32) + after[at, rows].astype(f32)
+                    ).astype(bf16)
+                    return carry
+
+                lax.fori_loop(0, half, next_sum, 0)
+            away = 1 - steps[step + 1][0]
+            half = after.shape[0] // 2
+            flying[chunk] = push(step + 1, chunk, after.at[pl.ds(away * half, half), rows])
+        held = after
 
 
 def scatter_blocks(blocks, clips, frames):
     count, rows, columns = blocks.shape
     clip_bits, frame_bits = clips.bit_length() - 1, frames.bit_length() - 1
     steps = clip_bits + frame_bits
+    units = rows // 16
+    parts = min(4, units)
+    edges = [units * part // parts * 16 for part in range(parts + 1)]
+    chunks = [(first, last - first) for first, last in zip(edges[:-1], edges[1:])]
     arrivals = [pltpu.VMEM((clips // 2, frames, rows, columns), bf16)]
     for step in range(1, steps):
         arrivals.append(pltpu.VMEM((count >> (step + 1), rows, columns), bf16))
     return pl.pallas_call(
-        functools.partial(scatter_kernel, clip_bits, frame_bits),
+        functools.partial(scatter_kernel, clip_bits, frame_bits, chunks),
         out_shape=jax.ShapeDtypeStruct((rows, columns), f32),
         in_specs=[pl.BlockSpec(memory_space=pltpu.VMEM)],
         out_specs=pl.BlockSpec(memory_space=pltpu.VMEM),
         scratch_shapes=[pltpu.VMEM((count // 2, rows, columns), bf16)]
         + arrivals
-        + [pltpu.SemaphoreType.DMA((steps,)), pltpu.SemaphoreType.DMA((steps,))],
+        + [pltpu.SemaphoreType.DMA((steps, parts))] * 2,
         compiler_params=pltpu.CompilerParams(
             collective_id=1, has_side_effects=True, vmem_limit_bytes=52 * 2**20
         ),
@@ -211,13 +228,21 @@
         ends.append((ends[-1] if ends else 0) + size)
     wide = gather_rows(
         jnp.concatenate(
-            [query_weight, key_weight, value_weight, output_weight, inner_weight, small], axis=1
+            [
+                query_weight,
+                key_weight,
+                value_weight,
+                output_weight,
+                inner_weight,
+                small,
+                outer_weight.reshape(own, -1),
+            ],
+            axis=1,
         )
     )
-    wide, outer_weight = lax.optimization_barrier((wide, outer_weight))
-    outer_mat = gather_rows(outer_weight)
-    (query_mat, key_mat, value_mat, proj_mat, inner_mat, shared) = jnp.split(wide, ends[:-1], axis=1)
+    (query_mat, key_mat, value_mat, proj_mat, inner_mat, shared, outer_mat) = jnp.split(wide, ends, axis=1)
     total = query_mat.shape[0]
+    outer_mat = outer_mat.reshape(-1, outer_weight.shape[1])
     (pre_gain, pre_shift, query_add, value_add, proj_add, post_gain, post_shift, outer_add) = [
         shared[:, at] for at in range(8)
     ]

time: 431 us -> 380 us (0.88)
  waiting for transfers between devices: 182 us -> 145 us
  Pallas kernels: 129 us -> 106 us
  local copies, waits for them, and re-layouts: 42.4 us -> 56.7 us
    all_gather x2 -> x1, waiting for transfers between devices: 130 us -> 107 us  [gather_rows(): return lax.all_gather(part, AXES, axis=0, tiled=True)]
    pallas_call x1, Pallas kernels: 129 us -> 106 us  [scatter_blocks(): pl.pallas_call(functools.partial(scatter_kernel, clip_bits, frame_bits, c...]
    all_gather x1, waiting for transfers between devices: 30.3 us -> 17.3 us  [body(): lax.all_gather(jnp.concatenate([keys, values], axis=1), 'frame', axis=0,...]
    reshape x0 -> x2, local copies, waits for them, and re-layouts: none -> 9.5 us  [the longest x1 8.49 us: body(): outer_mat = outer_mat.reshape(-1, outer_weight.shape[1])]
    split x0 -> x1, local copies, waits for them, and re-layouts: none -> 5.08 us  [body(): jnp.split(wide, ends, axis=1)]
    unnamed x5 -> x4, waiting for transfers between devices: 21.8 us -> 20.8 us
    unnamed x128 -> x129, local copies, waits for them, and re-layouts: 20.9 us -> 20.6 us
  transfers between devices with their start and end apart: 4 -> 3, of which waited for: 4 -> 3; matrix products, arithmetic and copies ran while one was open for 8% -> 8% of each run, Pallas kernels for 0% -> 0%
where the time goes in v3:
time: 380 us; the launch traced here: 378 us
  waiting for transfers between devices  145 us (38%)
  Pallas kernels  106 us (28%)
  local copies, waits for them, and re-layouts  56.7 us (15%)
  matrix products  46.3 us (12%)
  between operations  14.7 us (4%)
  other arithmetic  10.4 us (3%)
    all_gather x1, waiting for transfers between devices, gather_rows(): return lax.all_gather(part, AXES, axis=0, tiled=True)  107 us
    pallas_call x1, Pallas kernels, scatter_blocks(): pl.pallas_call(functools.partial(scatter_kernel, clip_bits, frame_bits, c...  106 us
    unnamed x4, waiting for transfers between devices  20.8 us
    unnamed x129, local copies, waits for them, and re-layouts  20.6 us
    all_gather x1, waiting for transfers between devices, body(): lax.all_gather(jnp.concatenate([keys, values], axis=1), 'frame', axis=0,...  17.3 us
    dot_general x6, matrix products, matmul(): return jnp.dot(left, right, preferred_element_type=jnp.float32)  15.8 us
    dot_general x6, matrix products, right_product(): jnp.einsum('to,io->ti', left, right, preferred_element_type=jnp.float32)  15.5 us
    reshape x1, local copies, waits for them, and re-layouts, body(): outer_mat = outer_mat.reshape(-1, outer_weight.shape[1])  8.49 us
  transfers between devices with their start and end apart: 3, of which 3 were waited for; matrix products, arithmetic and copies ran while one was open for 8% of the time, Pallas kernels for 0%

profile of v3, /device:TPU:0, one launch (start us, length us, event | category | flops | bytes accessed | tf_op | source)
XLA Modules:
  0.0 378.3 jit_solution(2231716092416378711)
XLA Ops:
  7.2 0.8 constant_dynamic-update-slice_fusion.6
  8.1 0.7 reshape.284
  8.8 0.8 concatenate.40
  9.7 1.0 reshape.285
  10.7 0.8 constant_dynamic-update-slice_fusion.5
  11.5 0.8 constant_dynamic-update-slice_fusion.4
  12.3 0.8 constant_dynamic-update-slice_fusion.3
  13.0 0.9 constant_dynamic-update-slice_fusion.2
  14.0 0.7 copy-done.29
  15.2 106.5 %all-gather.3.cloned.1.call-done = bf16[768,9344]{1,0:T(8,128)(2,1)} async-done(((bf16[24,9344]{1,0:T(8,128)(2,1)}), bf16[768,9344]{1,0:T(8,128)(2,1)}) %all-gather.3.cloned.1.call-update) | async-done | bytes 14352400 | tf_op jit(solution)/shard_map/all_gather | solution.py:60
  121.7 3.7 convert_reduce_fusion.1
  125.4 1.6 convolution_convert_fusion.10
  127.1 1.6 fusion.31
  128.8 0.8 pad_maximum_fusion.1
  129.6 1.7 fusion.30
  131.3 0.8 copy.65
  132.1 1.0 slice.190
  133.4 0.7 reshape.304
  134.2 5.1 %split.30 = bf16[768,3072]{1,0:T(8,128)(2,1)} slice(bf16[768,9344]{1,0:T(8,128)(2,1)} %all-gather.3.cloned.1.call-done), slice={[0:768], [6272:9344]} | slice | bytes 9437184 | tf_op jit(solution)/shard_map/split | solution.py:243
  139.2 8.5 %reshape.289 = bf16[3072,768]{1,0:T(8,128)(2,1)} reshape(bf16[768,3072]{1,0:T(8,128)(2,1)} %split.30) | data formatting | bytes 9437184 | tf_op jit(solution)/shard_map/reshape | solution.py:245
  147.7 17.3 %all-gather.5.cloned.1.call-done = bf16[512,1536]{1,0:T(8,128)(2,1)} async-done(((bf16[128,1536]{1,0:T(8,128)(2,1)}), bf16[512,1536]{1,0:T(8,128)(2,1)}) %all-gather.5.cloned.1.call-update) | async-done | bytes 1572880 | tf_op jit(solution)/shard_map/all_gather | solution.py:261
  165.0 1.5 fusion.76
  166.5 1.2 copy.64
  167.6 1.2 copy.66
  168.8 1.9 fusion.80
  170.8 0.8 exponential_reduce_fusion
  171.9 0.8 convolution_convert_fusion.9
  172.8 1.9 fusion.81
  175.0 7.5 %fusion.11 = (bf16[128,3072]{1,0:T(8,128)(2,1)}, f32[128,3072]{1,0:T(8,128)S(1)}) fusion(f32[3072]{0:T(1024)S(1)} %copy-done.38, bf16[768,9344]{1,0:T(8,128)(2,1)} %all-gather.3.cloned.1.call-done, f32[128,768]{1,0:T(8,128)S(1)} %get-tuple-element.63, f32[768]{0:T(1024)S(1)} %copy-done.30, f32[768]{0:T(1024)S(1)} %get-tuple-element.19, ...), kind=kOutput, calls=%fused_computation.17 | convolution fusion | flops 630423552 | bytes 7490560 | tf_op jit(solution)/shard_map/dot_general | solution.py:39
  182.5 2.4 fusion.82
  184.8 5.0 %multiply_reduce_fusion = (bf16[768]{0:T(1024)(128)(2,1)}, f32[128]{0:T(128)S(1)}, f32[128]{0:T(128)S(1)}, bf16[768]{0:T(1024)(128)(2,1)}, f32[128,768]{1,0:T(8,128)S(1)}) fusion(f32[128,768]{1,0:T(8,128)S(1)} %get-tuple-element.63, f32[128]{0:T(128)S(1)} %add_rsqrt_fusion, f32[128]{0:T(128)S(1)} %broadcast_multiply_fusion.4, ...), kind=kOutput, calls=%fused_computation.100 | convolution fusion | flops 604862720 | bytes 6299648 | tf_op jit(solution)/shard_map/to,io->ti/dot_general | solution.py:47
  189.8 0.8 fusion.74
  190.6 0.8 copy-done.9
  191.4 2.5 convolution_convert_fusion.8
  193.9 1.7 copy.68
  195.6 1.1 fusion.58
  196.7 1.8 convolution_convert_fusion.6
  198.5 1.3 multiply_convert_fusion
  199.8 1.2 copy-done.1
  201.5 1.6 copy.91
  203.3 1.2 copy-done.2
  205.8 1.8 fusion.34
  207.6 3.6 convolution_convert_fusion
  211.3 1.5 convolution_convert_fusion.1
  212.8 2.3 fusion.75
  215.1 1.5 fusion.29
  216.6 20.8 %reduce-scatter.4.cloned.1.call-done = bf16[128,1536]{1,0:T(8,128)(2,1)} async-done(((bf16[512,1536]{1,0:T(8,128)(2,1)}), bf16[128,1536]{1,0:T(8,128)(2,1)}) %reduce-scatter.4.cloned.1.call-update) | async-done | bytes 393232
  237.4 2.0 convolution_add_fusion.1
  239.4 1.9 convolution_add_fusion
  241.3 0.7 copy-done.16
  242.1 0.8 fusion.56
  242.9 0.8 copy.69
  244.3 0.8 copy.79
  245.1 1.3 pad.10
  246.5 2.5 copy.80
  248.9 1.5 fusion.24
  252.5 0.9 copy-done.15
  254.0 0.9 copy-done.13
  255.8 0.8 copy-done.21
  256.7 5.3 %copy-done = bf16[32,304,768]{2,1,0:T(8,128)(2,1)} copy-done((bf16[32,304,768]{2,1,0:T(8,128)(2,1)}, bf16[32,304,768]{2,1,0:T(8,128)(2,1)S(1)}, u32[]{:S(2)}) %copy-start) | copy-done | bytes 14942232
  261.9 105.5 %shard_map.296 = f32[304,768]{1,0:T(8,128)S(1)} custom-call(bf16[4,2,4,304,768]{4,3,2,1,0:T(8,128)(2,1)} %bitcast.94), custom_call_target="tpu_custom_call" | custom-call | tf_op jit(solution)/shard_map/pallas_call | solution.py:170
  369.4 0.7 slice.179
  370.2 0.9 fusion.55
  371.0 0.7 pad_maximum_fusion.2
  (161 shorter events, 9.5 us)
Async XLA Ops:
  7.2 7.6 %copy-start.3 = (bf16[128,768]{1,0:T(8,128)(2,1)S(1)}, bf16[128,768]{1,0:T(8,128)(2,1)}, u32[]{:S(2)}) copy-start(bf16[128,768]{1,0:T(8,128)(2,1)} %param.17) | copy-start | bytes 589828
  7.2 114.5 %all-gather.3.cloned.1.call-start = ((), (), s32[]{:S(2)}) async-start(), calls=%async_computation.1 | async-start | bytes 14800896 | tf_op jit(solution)/shard_map/all_gather | solution.py:60
  14.0 0.8 copy-start.29
  14.8 150.2 %all-gather.5.cloned.1.call-start = ((), (), s32[]{:S(2)}) async-start(), calls=%async_computation.2 | async-start | bytes 1966080 | tf_op jit(solution)/shard_map/all_gather | solution.py:261
  15.0 114.7 %copy-start.36 = (f32[128]{0:T(128)}, f32[128]{0:T(128)S(1)}, u32[]{:S(2)}) copy-start(f32[128]{0:T(128)S(1)} %broadcast_multiply_fusion.5) | copy-start | bytes 1540
  15.2 114.4 %copy-start.39 = (f32[128]{0:T(128)}, f32[128]{0:T(128)S(1)}, u32[]{:S(2)}) copy-start(f32[128]{0:T(128)S(1)} %add_rsqrt_fusion.1) | copy-start | bytes 1540
  125.4 4.2 %copy-start.32 = (f32[768]{0:T(1024)}, f32[768]{0:T(1024)S(1)}, u32[]{:S(2)}) copy-start(f32[768]{0:T(1024)S(1)} %get-tuple-element.23) | copy-start | bytes 9220
  129.6 107.8 %reduce-scatter.4.cloned.1.call-start = ((), (), s32[]{:S(2)}) async-start(), calls=%async_computation.3 | async-start | bytes 1966080
  170.8 1.1 copy-start.7
  171.9 0.9 copy-start.4
  171.9 0.9 copy-start.34
  172.7 2.0 copy-start.19
  172.7 2.3 copy-start.30
  172.7 2.3 copy-start.38
  172.8 9.6 %slice-start.2 = ((s8[4718592]{0:T(1024)(128)(4,1)}), s8[4194304]{0:T(1024)(128)(4,1)S(1)}, s32[]{:S(2)}) async-start(s8[4718592]{0:T(1024)(128)(4,1)} %bitcast.90), calls=%async_computation.6 | async-start | bytes 8388608
  174.7 15.1 %copy-start.41 = (f32[128]{0:T(128)}, f32[128]{0:T(128)S(1)}, u32[]{:S(2)}) copy-start(f32[128]{0:T(128)S(1)} %broadcast_multiply_fusion.4) | copy-start | bytes 1540
  174.9 14.9 %copy-start.45 = (f32[128]{0:T(128)}, f32[128]{0:T(128)S(1)}, u32[]{:S(2)}) copy-start(f32[128]{0:T(128)S(1)} %add_rsqrt_fusion) | copy-start | bytes 1540
  175.0 7.5 %slice-start.3 = ((s8[4718592]{0:T(1024)(128)(4,1)}), s8[524288]{0:T(1024)(128)(4,1)S(1)}, s32[]{:S(2)}) async-start(s8[4718592]{0:T(1024)(128)(4,1)} %bitcast.90), calls=%async_computation.7 | async-start | bytes 1048576
  175.0 7.5 %copy-start.25 = (bf16[128,768]{1,0:T(8,128)(2,1)S(1)}, bf16[128,768]{1,0:T(8,128)(2,1)}, u32[]{:S(2)}) copy-start(bf16[128,768]{1,0:T(8,128)(2,1)} %param.33) | copy-start | bytes 589828
  184.8 5.0 %copy-start.27 = (bf16[128,3072]{1,0:T(8,128)(2,1)}, bf16[128,3072]{1,0:T(8,128)(2,1)S(1)}, u32[]{:S(2)}) copy-start(bf16[128,3072]{1,0:T(8,128)(2,1)S(1)} %get-tuple-element.69) | copy-start | bytes 2359300
  190.6 0.8 copy-start.9
  196.7 1.8 copy-start.8
  196.7 1.8 copy-start.18
  198.5 2.5 copy-start.24
  199.8 1.2 copy-start.1
  201.4 1.7 copy-start.26
  201.4 1.9 copy-start.6
  203.1 1.4 copy-start.2
  203.1 2.2 copy-start.43
  203.1 2.3 copy-start.48
  203.1 2.4 copy-start.47
  203.2 2.5 copy-start.44
  205.2 2.4 copy-start.11
  207.6 3.7 copy-start.28
  207.6 3.7 copy-start.31
  207.6 3.6 copy-start.42
  207.6 3.6 copy-start.46
  211.3 3.9 %slice-start.4 = ((s8[4718592]{0:T(1024)(128)(4,1)}), s8[4194304]{0:T(1024)(128)(4,1)S(1)}, s32[]{:S(2)}) async-start(s8[4718592]{0:T(1024)(128)(4,1)} %bitcast.92), calls=%async_computation.8 | async-start | bytes 8388608
  212.8 2.3 slice-start.5
  212.8 2.3 copy-start.35
  237.4 2.0 copy-start.22
  239.4 2.7 copy-start.5
  239.4 2.7 copy-start.33
  239.4 2.7 copy-start.37
  239.4 2.7 copy-start.40
  241.3 0.8 copy-start.16
  248.9 1.5 copy-start.23
  251.0 1.0 copy-start.10
  251.0 1.0 copy-start.20
  251.1 4.3 %slice-start = ((s8[4718592]{0:T(1024)(128)(4,1)}), s8[4194304]{0:T(1024)(128)(4,1)S(1)}, s32[]{:S(2)}) async-start(s8[4718592]{0:T(1024)(128)(4,1)} %bitcast.87), calls=%async_computation.4 | async-start | bytes 8388608
  251.8 1.7 copy-start.15
  252.5 1.4 copy-start.14
  253.4 2.0 slice-start.1
  253.5 1.4 copy-start.13
  254.0 1.4 copy-start.12
  255.5 1.1 copy-start.21
  256.7 5.3 %copy-start = (bf16[32,304,768]{2,1,0:T(8,128)(2,1)}, bf16[32,304,768]{2,1,0:T(8,128)(2,1)S(1)}, u32[]{:S(2)}) copy-start(bf16[32,304,768]{2,1,0:T(8,128)(2,1)S(1)} %constant_dynamic-update-slice_fusion.7) | copy-start | bytes 44826628
  367.4 2.7 copy-start.50
  367.5 2.7 copy-start.49
  367.5 2.7 copy-start.17
Sparse Core Ops, SparseCore 0:
  14.9 106.7 all-gather.2
  129.7 35.2 all-gather.4
  203.2 34.1 reduce-scatter.3
